TPU v7x, 256 devices: a whole 4x4x8 slice. The times are simulated.
256 devices in a mesh: dp: 8 (over z), ctx: 32 (over y, x, core).
Axes of the slice: x: 4, y: 4, z: 8, core: 2. Of those that a mesh axis runs over, the one named last changes fastest.
Arguments:
- inputs: bfloat16 [8, 4096, 3072], P('dp', 'ctx'), may hold values from -0.0625 to 0.0625
- queries: bfloat16 [8, 4096, 4096], P('dp', 'ctx'), may hold values from -0.625 to 0.625
- keys: bfloat16 [8, 4096, 4096], P('dp', 'ctx'), may hold values from -0.625 to 0.625
- values: bfloat16 [8, 4096, 4096], P('dp', 'ctx'), may hold values from -0.625 to 0.625
- out_grad: bfloat16 [8, 4096, 4096], P('dp', 'ctx'), may hold values from -0.625 to 0.625
- log_gate: float32 [8, 32, 4096], P('dp', None, 'ctx'), may hold values from -1 to 0
- boundaries: int32 [8, 4], P('dp'), may hold values from 1 to 4095, as said below
Outputs:
- query_grad: bfloat16 [8, 4096, 4096], P('dp', 'ctx')
- key_grad: bfloat16 [8, 4096, 4096], P('dp', 'ctx')
- value_weight_grad: float32 [3072, 4096], P('ctx', 'dp')
Inputs may be any that keep to these rules, and one draw needn't show every extreme that they name: `boundaries`: boundary j of a sequence (counting from 0) lies between j * 1024 + 1 and j * 1024 + 1023.
All inputs are finite; a program needn't handle non-finite values.
Results may differ from a plain program's by a relative error of at most 0.034.
Values may be sent and summed in bfloat16 or wider, within the bound.
No kernel may reach another device: no remote copies, remote signals or barrier semaphores. Data moves between devices by JAX's collectives and lax.ppermute only.
A program may use at most 192 MiB of HBM per device.

v0:
```python
import functools
import itertools

import jax
import jax.numpy as jnp
from jax import lax
from jax.experimental import pallas as pl
from jax.experimental.pallas import tpu as pltpu
from jax.sharding import Mesh
from jax.sharding import PartitionSpec as P

F32, BF16 = jnp.float32, jnp.bfloat16
HEAD = 128
TOK = 128
PAIR = 2 * TOK
LINE = 8
SPAN = 4
OWN = 16
PART = OWN // SPAN
STATE = PART * HEAD
TAIL = 16
CTX = ("y", "x", "core")
VMEM_LIMIT = 16 << 20
HEAVY = 33
WEIGHTS = (32, 31)
CUTS = (0, 6, 8)


def mm(a, b, lhs, rhs):
    return lax.dot_general(a, b, (((lhs,), (rhs,)), ((), ())), preferred_element_type=F32)


def segment_of(bounds_ref, positions):
    total = jnp.zeros_like(positions)
    for j in range(bounds_ref.shape[0]):
        total = total + (bounds_ref[j] <= positions).astype(jnp.int32)
    return total


def scalar_segment(bounds_ref, position):
    total = jnp.int32(0)
    for j in range(bounds_ref.shape[0]):
        total = total + (bounds_ref[j] <= position).astype(jnp.int32)
    return total


def enter_columns(cum_t, bounds_ref, begin):
    positions = begin + lax.broadcasted_iota(jnp.int32, cum_t.shape, 0)
    same = segment_of(bounds_ref, positions) == scalar_segment(bounds_ref, begin - 1)
    return jnp.where(same, jnp.exp(cum_t), 0.0)


def leave_columns(cum_t, bounds_ref, begin):
    positions = begin + lax.broadcasted_iota(jnp.int32, cum_t.shape, 0)
    same = segment_of(bounds_ref, positions) == scalar_segment(bounds_ref, begin + PAIR - 1)
    return jnp.where(same, jnp.exp(cum_t[PAIR - 1 :, :] - cum_t), 0.0)


def head_cut(h):
    return slice(h * HEAD, (h + 1) * HEAD)


def pick_kernel(place_ref, gate_ref, *refs):
    core = place_ref[1]
    sources, (gate_keep, gate_send, keep_ref, send_ref) = refs[:4], refs[4:]
    for d in range(LINE):
        gate_keep[2 * d : 2 * d + 2, :] = gate_ref[2 * d + core]
        gate_send[2 * d : 2 * d + 2, :] = gate_ref[2 * d + 1 - core]
        for target, who in ((keep_ref, core), (send_ref, 1 - core)):
            lanes = pl.ds(pl.multiple_of((2 * d + who) * 2 * HEAD, 2 * HEAD), 2 * HEAD)
            for n, source in enumerate(sources):
                target[n, :, 2 * d * HEAD : 2 * (d + 1) * HEAD] = source[:, lanes]


def turn_kernel(x_ref, out_ref, hold):
    for j in range(x_ref.shape[1] // TOK):
        hold[j * TOK : (j + 1) * TOK, :] = x_ref[:, j * TOK : (j + 1) * TOK].T
    count, near = out_ref.shape[1:3]
    for j in range(count):
        for core in range(2):
            out_ref[core, j] = hold[(2 * j + core) * near : (2 * j + core + 1) * near, :]


def pair_kernel(place_ref, keep_ref, other_ref, out_ref):
    first = place_ref[1] == 0
    for half in range(2):
        keep, other = keep_ref[half], other_ref[half]
        out_ref[half, :, :TOK] = jnp.where(first, keep, other)
        out_ref[half, :, TOK:] = jnp.where(first, other, keep)


def other_kernel(place_ref, block_ref, out_ref):
    out_ref[...] = block_ref[1 - place_ref[1]]


def join(core, n, keep_ref, other_ref, out_ref):
    out_ref[pl.ds(pl.multiple_of(core * TOK, TOK), TOK), :] = keep_ref[n]
    out_ref[pl.ds(pl.multiple_of((1 - core) * TOK, TOK), TOK), :] = other_ref[n]


def states_kernel(place_ref, bounds_ref, *refs):
    gate_keep, gate_other, keep_ref, other_ref = refs[:4]
    out_refs, refs = refs[4 : 4 + SPAN], refs[4 + SPAN :]
    cum_ref, q_ref, g_ref, k_ref, v_ref, hold = refs
    begin, core = place_ref[0], place_ref[1]
    for n, ref in enumerate((q_ref, g_ref, k_ref, v_ref)):
        join(core, n, keep_ref, other_ref, ref)
    gates = (gate_keep[...], gate_other[...])
    swap = core == 1
    gate = jnp.concatenate(
        [jnp.where(swap, gates[1], gates[0]), jnp.where(swap, gates[0], gates[1])], axis=1
    )
    before = lax.broadcasted_iota(jnp.int32, (PAIR, PAIR), 0)
    after = lax.broadcasted_iota(jnp.int32, (PAIR, PAIR), 1)
    cum = jnp.dot(
        gate,
        (before <= after).astype(F32),
        precision=lax.Precision.HIGHEST,
        preferred_element_type=F32,
    )
    for d in range(LINE):
        cum_ref[d] = cum[2 * d : 2 * d + 2, :]
    enter = enter_columns(cum.T, bounds_ref, begin)
    leave = leave_columns(cum.T, bounds_ref, begin)
    rows = lax.broadcasted_iota(jnp.int32, (TAIL, HEAD), 0)
    for o in range(SPAN):
        tail = jnp.zeros((TAIL, HEAD), F32)
        for j in range(PART):
            h = o * PART + j
            weighted = (enter[:, h : h + 1] * q_ref[:, head_cut(h)].astype(F32)).astype(BF16)
            hold[o, head_cut(j), :] = mm(weighted, g_ref[:, head_cut(h)], 0, 0).astype(BF16)
            weighted = (leave[:, h : h + 1] * k_ref[:, head_cut(h)].astype(F32)).astype(BF16)
            hold[o, head_cut(PART + j), :] = mm(weighted, v_ref[:, head_cut(h)], 0, 0).astype(BF16)
            tail = jnp.where(rows == j, enter[PAIR - 1 :, h : h + 1], tail)
        hold[o, 2 * STATE :, :] = tail.astype(BF16)
    send_apart(place_ref[3], hold, out_refs)


def columns_of(cum_ref):
    return jnp.concatenate([cum_ref[d] for d in range(cum_ref.shape[0])], axis=0).T


def send_apart(place, hold, out_refs):
    for step, out_ref in enumerate(out_refs):
        out_ref[...] = hold[lax.rem(place + step, len(out_refs))]


def advance(state, hold, block, backward):
    pieces = []
    for j in range(PART):
        through = hold[block, 2 * STATE + j : 2 * STATE + j + 1, :].astype(F32)
        part = hold[block, head_cut(j if backward else PART + j), :].astype(F32)
        pieces.append(through * state[head_cut(j)] + part)
    return jnp.concatenate(pieces, axis=0)


def walk(backward):
    return reversed(range(SPAN)) if backward else range(SPAN)


def total_kernel(place_ref, *refs):
    parts, (back_ref, front_ref, sorted_ref) = refs[:SPAN], refs[SPAN:]
    take_in(place_ref[3], parts, sorted_ref)
    for backward, total_ref in ((True, back_ref), (False, front_ref)):
        state = jnp.zeros((STATE, HEAD), F32)
        for block in walk(backward):
            state = advance(state, sorted_ref, block, backward)
        total_ref[...] = state.astype(BF16)


def carry_kernel(place_ref, sorted_ref, back_ref, front_ref, *refs):
    out_refs, hold = refs[:SPAN], refs[SPAN]
    for backward, entry_ref in ((True, back_ref), (False, front_ref)):
        state = entry_ref[...].astype(F32)
        cut = slice(0, STATE) if backward else slice(STATE, 2 * STATE)
        for block in walk(backward):
            hold[block, cut, :] = state.astype(BF16)
            state = advance(state, sorted_ref, block, backward)
    send_apart(place_ref[3], hold, out_refs)


def take_in(lane, parts, hold):
    for step, part in enumerate(parts):
        hold[lax.rem(lane - step + SPAN, SPAN)] = part[...]


def inner_kernel(place_ref, bounds_ref, cum_ref, *refs):
    q_ref, k_ref, v_ref, g_ref, query_ref, key_ref, value_ref = refs
    begin = place_ref[0]
    cum = cum_ref[...]
    cum_t = cum.T
    row = lax.broadcasted_iota(jnp.int32, (PAIR, PAIR), 0)
    column = lax.broadcasted_iota(jnp.int32, (PAIR, PAIR), 1)
    row_ids = segment_of(bounds_ref, begin + lax.broadcasted_iota(jnp.int32, (PAIR, 1), 0))
    column_ids = segment_of(bounds_ref, begin + lax.broadcasted_iota(jnp.int32, (1, PAIR), 1))
    causal = (row >= column) & (row_ids == column_ids)
    for h in range(cum.shape[0]):
        cut = head_cut(h)
        decay = jnp.exp(jnp.where(causal, cum_t[:, h : h + 1] - cum[h : h + 1, :], -1e30))
        q, k, v, g = q_ref[:, cut], k_ref[:, cut], v_ref[:, cut], g_ref[:, cut]
        score_grad = (decay * mm(g, v, 1, 1)).astype(BF16)
        score_keys = (decay * mm(q, k, 1, 1)).astype(BF16)
        query_ref[:, cut] = mm(score_grad, k, 1, 0)
        key_ref[:, cut] = mm(score_grad, q, 0, 0)
        value_ref[:, cut] = mm(score_keys, g, 0, 0)


def piece_of(parts, h):
    for low, high, part in zip(CUTS, CUTS[1:], parts):
        if low <= h // 2 < high:
            return part[:, head_cut(h - 2 * low)]


def value_kernel(place_ref, bounds_ref, cum_ref, k_ref, *refs):
    value_in, states, refs = refs[:2], refs[2 : 2 + SPAN], refs[2 + SPAN :]
    send_ref, keep_ref, hold, out_hold = refs
    core, deep = place_ref[1], place_ref[2]
    take_in(place_ref[3], states, hold)
    leave = leave_columns(columns_of(cum_ref), bounds_ref, place_ref[0])
    for h in range(OWN):
        state = hold[h // PART, head_cut(h % PART), :]
        extra = leave[:, h : h + 1] * mm(k_ref[:, head_cut(h)], state, 1, 0)
        out_hold[h // 2, :, head_cut(h % 2)] = (piece_of(value_in, h) + extra).astype(BF16)
    keep_ref[LINE // 2 - 1] = out_hold[deep]
    send_ref[LINE // 2 - 1] = out_hold[deep]
    keep_ref[LINE // 2] = out_hold[lax.rem(deep + LINE // 2, LINE)]
    for n in range(LINE // 2 - 1):
        ahead, behind = lax.rem(deep + 1 + n, LINE), lax.rem(deep + LINE - 1 - n, LINE)
        keep_ref[n] = out_hold[jnp.where(core == 0, ahead, behind)]
        send_ref[n] = out_hold[jnp.where(core == 0, behind, ahead)]


def bundle_kernel(keep_ref, other_ref, *out_refs):
    for n, out_ref in enumerate(out_refs[:-1]):
        out_ref[0] = keep_ref[n]
        out_ref[1] = other_ref[n]
    out_refs[-1][...] = keep_ref[len(out_refs) - 1]


def part_rows(core, value, cut, keep_ref, send_ref):
    keep_ref[:, cut] = jnp.where(core == 0, value[:TOK], value[TOK:]).astype(BF16)
    send_ref[:, cut] = jnp.where(core == 0, value[TOK:], value[:TOK]).astype(BF16)


def key_kernel(place_ref, bounds_ref, cum_ref, v_ref, *refs):
    key_in, states, (keep_ref, send_ref, hold) = refs[:2], refs[2 : 2 + SPAN], refs[2 + SPAN :]
    take_in(place_ref[3], states, hold)
    leave = leave_columns(columns_of(cum_ref), bounds_ref, place_ref[0])
    for h in range(OWN):
        state = hold[h // PART, head_cut(h % PART), :]
        extra = leave[:, h : h + 1] * mm(v_ref[:, head_cut(h)], state, 1, 1)
        part_rows(place_ref[1], piece_of(key_in, h) + extra, head_cut(h), keep_ref, send_ref)


def query_kernel(place_ref, bounds_ref, cum_ref, g_ref, *refs):
    query_in, states, (keep_ref, send_ref, hold) = refs[:2], refs[2 : 2 + SPAN], refs[2 + SPAN :]
    take_in(place_ref[3], states, hold)
    enter = enter_columns(columns_of(cum_ref), bounds_ref, place_ref[0])
    for h in range(OWN):
        state = hold[h // PART, head_cut(PART + h % PART), :]
        extra = enter[:, h : h + 1] * mm(g_ref[:, head_cut(h)], state, 1, 1)
        part_rows(place_ref[1], piece_of(query_in, h) + extra, head_cut(h), keep_ref, send_ref)


def lay_kernel(place_ref, keep_ref, other_ref, out_ref):
    core = place_ref[1]
    for d in range(LINE):
        near = slice(2 * d * HEAD, 2 * (d + 1) * HEAD)
        for source, who in ((keep_ref, core), (other_ref, 1 - core)):
            lanes = pl.ds(pl.multiple_of((2 * d + who) * 2 * HEAD, 2 * HEAD), 2 * HEAD)
            out_ref[:, lanes] = source[:, near]


def by_core(place_ref, keep, other):
    first = place_ref[1] == 0
    return jnp.concatenate([jnp.where(first, keep, other), jnp.where(first, other, keep)], axis=1)


def part_out(place_ref, rows, right, out_refs, hold):
    first, x, y = place_ref[1] == 0, place_ref[3], place_ref[4]
    near = hold.shape[1]
    tall = SPAN * near
    for j in range(SPAN):
        cut = slice(j * tall, (j + 1) * tall)
        acc = mm(rows[0][cut, :], right[0], 1, 0)
        for row, column in zip(rows[1:], right[1:], strict=True):
            acc = acc + mm(row[cut, :], column, 1, 0)
        acc = acc.astype(BF16)
        for i in range(SPAN):
            hold[j * SPAN + i] = acc[i * near : (i + 1) * near]
    for step, out_ref in enumerate(out_refs):
        there_x, there_y = lax.rem(x + step, SPAN), lax.rem(y + step, SPAN)
        for n in range(SPAN):
            out_ref[n] = hold[jnp.where(first, n * SPAN + there_x, there_y * SPAN + n)]


def mine_kernel(place_ref, block_ref, out_ref):
    out_ref[...] = block_ref[place_ref[1]]


def weight_kernel(place_ref, *refs):
    count = LINE // 2 - 1
    own_row, heres, theres, refs = refs[0], refs[1 : 1 + count], refs[1 + count : 1 + 2 * count], refs[1 + 2 * count :]
    far_row, far, far_other = refs[:3]
    own, near_refs, refs = refs[3], refs[4 : 4 + 2 * count], refs[4 + 2 * count :]
    core = place_ref[1]
    rows, right = [own_row.at[core]], [by_core(place_ref, own[0], own[1])]
    for n in range(count):
        here, there = near_refs[2 * n], near_refs[2 * n + 1]
        rows += [heres[n].at[core], theres[n]]
        right.append(by_core(place_ref, here[0], here[1]))
        right.append(by_core(place_ref, there[1], there[0]))
    rows.append(far_row)
    right.append(by_core(place_ref, far[...], far_other[...]))
    part_out(place_ref, rows, right, refs[:SPAN], refs[SPAN])


def halfway_kernel(place_ref, *refs):
    parts, out_refs, hold = refs[:SPAN], refs[SPAN : 2 * SPAN], refs[2 * SPAN]
    for n in range(SPAN):
        total = parts[0][n].astype(F32)
        for part in parts[1:]:
            total = total + part[n].astype(F32)
        hold[n] = total.astype(BF16)
    send_apart(jnp.where(place_ref[1] == 0, place_ref[4], place_ref[3]), hold, out_refs)


def sum_kernel(*refs):
    parts, out_ref = refs[:-1], refs[-1]
    total = parts[0][...].astype(F32)
    for part in parts[1:]:
        total = total + part[...].astype(F32)
    out_ref[...] = total.astype(out_ref.dtype)


def shape(dims, dtype=BF16):
    return jax.ShapeDtypeStruct(dims, dtype)


def cost(heavy=0):
    return pl.CostEstimate(
        flops=1 << heavy, bytes_accessed=1, transcendentals=0
    )


def held(values, after):
    spec = pl.BlockSpec(memory_space=pl.ANY)
    return pl.pallas_call(
        lambda *refs: None,
        in_specs=[spec] * (len(values) + len(after)),
        out_specs=[spec] * len(values),
        out_shape=[shape(v.shape, v.dtype) for v in values],
        input_output_aliases={n: n for n in range(len(values))},
        compiler_params=pltpu.CompilerParams(vmem_limit_bytes=VMEM_LIMIT),
        cost_estimate=cost(),
    )(*values, *after)


def whole(kernel, smem, arrays, outs, scratch=(), after=(), heavy=0):
    vmem = pl.BlockSpec(memory_space=pltpu.VMEM)
    count = len(smem) + len(arrays)

    def body(*refs):
        kernel(*refs[:count], *refs[count + len(after) :])

    return pl.pallas_call(
        body,
        in_specs=[pl.BlockSpec(memory_space=pltpu.SMEM)] * len(smem)
        + [vmem] * len(arrays)
        + [pl.BlockSpec(memory_space=pl.ANY)] * len(after),
        out_specs=[vmem] * len(outs),
        out_shape=outs,
        scratch_shapes=list(scratch),
        compiler_params=pltpu.CompilerParams(vmem_limit_bytes=VMEM_LIMIT),
        cost_estimate=cost(heavy),
    )(*smem, *arrays, *after)


def inner(part, smem, cum, arrays, after):
    low, high = CUTS[part], CUTS[part + 1]
    outs = [shape((PAIR, (high - low) * 2 * HEAD), F32)] * 3
    count = len(smem) + 1 + len(arrays)

    def body(*refs):
        inner_kernel(*refs[:count], *refs[count + len(after) :])

    return pl.pallas_call(
        body,
        grid=(high - low,),
        in_specs=[pl.BlockSpec(memory_space=pltpu.SMEM)] * len(smem)
        + [pl.BlockSpec((None, 2, PAIR), lambda d: (d + low, 0, 0))]
        + [pl.BlockSpec((PAIR, 2 * HEAD), lambda d: (0, d + low))] * len(arrays)
        + [pl.BlockSpec(memory_space=pl.ANY)] * len(after),
        out_specs=[pl.BlockSpec((PAIR, 2 * HEAD), lambda d: (0, d))] * len(outs),
        out_shape=outs,
        compiler_params=pltpu.CompilerParams(vmem_limit_bytes=VMEM_LIMIT),
        cost_estimate=cost(WEIGHTS[part]),
    )(*smem, cum, *arrays, *after)


def shifted(value, axis, step):
    count = lax.axis_size(axis)
    return lax.ppermute(value, axis, [(i, (i + step) % count) for i in range(count)])


def swapped(value):
    return shifted(value, "core", 1)


def exchange(pieces, axis):
    return [pieces[0]] + [shifted(pieces[s], axis, s) for s in range(1, len(pieces))]


def apart(value, axes, moves):
    sizes = [lax.axis_size(a) for a in axes]
    pairs = []
    for place in itertools.product(*map(range, sizes)):
        for core, move in enumerate(moves):
            there = [(p + m) % n for p, m, n in zip(place, move, sizes, strict=True)]
            index = lambda at: functools.reduce(lambda t, pn: t * pn[1] + pn[0], zip(at, sizes), 0)
            pairs.append((2 * index(place) + core, 2 * index(there) + core))
    return lax.ppermute(value, (*axes, "core"), pairs)


def per_device(inputs, queries, keys, values, out_grad, log_gate, boundaries):
    q, k, v, g = queries[0], keys[0], values[0], out_grad[0]
    width = q.shape[1]
    model = inputs.shape[2]
    core, x, y = lax.axis_index("core"), lax.axis_index("x"), lax.axis_index("y")
    begin = (y * lax.axis_size("x") + x) * PAIR
    place = jnp.stack([begin, core, lax.axis_index("z"), x, y]).astype(jnp.int32)
    smem = (place, boundaries[0])
    plane = lax.axis_size("y") * lax.axis_size("x")
    count = lax.axis_size("y")
    half, chip = shape((TOK, width // 2)), shape((PAIR, width // 2))
    gate_half, cums = shape((OWN, TOK), F32), shape((LINE, 2, PAIR), F32)
    state, span = shape((STATE, HEAD)), (SPAN, 2 * STATE + TAIL, HEAD)
    hold_states = pltpu.VMEM((SPAN, 2 * STATE, HEAD), BF16)

    line = shape((2, plane, model // plane // 2, TOK))
    (turned,) = whole(turn_kernel, (), [inputs[0]], [line], [pltpu.VMEM((model, TOK), BF16)])
    turned_other = swapped(turned)
    (own,) = whole(
        pair_kernel,
        (place,),
        [a.reshape(2, model // 2, TOK) for a in (turned, turned_other)],
        [shape((2, model // 2, PAIR))],
    )
    step = lambda block: apart(block, ("z",), [(1,), (-1,)])
    ring_1 = step(own)
    gate_keep, gate_send, keep, send = whole(
        pick_kernel,
        (place,),
        [log_gate[0].reshape(OWN, 2, TOK), q, g, k, v],
        [gate_half] * 2 + [shape((4, *half.shape))] * 2,
        after=[own],
        heavy=HEAVY,
    )
    *parts, cum, q, g, k, v = whole(
        states_kernel,
        smem,
        [gate_keep, swapped(gate_send), keep, swapped(send)],
        [shape(span[1:])] * SPAN + [cums] + [chip] * 4,
        [pltpu.VMEM(span, BF16)],
    )
    parts = exchange(parts, "x")
    inner_1 = inner(0, smem, cum, [q, k, v, g], [])
    parts = held(parts, [inner_1[0]])
    (ring_1,) = held([ring_1], [parts[1]])
    ring_2 = step(ring_1)
    back, front, parts = whole(total_kernel, (place,), parts, [state, state, shape(span)])
    back = lax.ppermute(back, "y", [(i + 1, i) for i in range(count - 1)])
    front = lax.ppermute(front, "y", [(i, i + 1) for i in range(count - 1)])
    carried = whole(
        carry_kernel,
        (place,),
        [parts, back, front],
        [shape((2 * STATE, HEAD))] * SPAN,
        [hold_states],
    )
    inner_2 = inner(1, smem, cum, [q, k, v, g], [carried[0]])
    carried = exchange(carried, "x")
    (ring_2,) = held([ring_2], [inner_2[0]])
    ring_3 = step(ring_2)
    carried = held(carried, [ring_2])
    query_in, key_in, value_in = zip(inner_1, inner_2)
    several = [shape((n, PAIR, 2 * HEAD)) for n in (LINE // 2, LINE // 2 + 1)]
    send, keep = whole(
        value_kernel,
        smem,
        [cum, k, *value_in, *carried],
        several,
        [hold_states, pltpu.VMEM((LINE, PAIR, 2 * HEAD), BF16)],
        heavy=HEAVY,
    )
    *bundles, own_part, far_part = whole(
        bundle_kernel,
        (),
        [keep, swapped(send)],
        [shape((2, PAIR, 2 * HEAD))] * (LINE // 2) + [shape((PAIR, 2 * HEAD))],
    )
    started = bundles[0]
    bundles = [apart(b, ("z",), [(n + 1,), (-n - 1,)]) for n, b in enumerate(bundles)]
    far_part = apart(far_part, ("z",), [(LINE // 2,), (LINE // 2,)])
    key_keep, key_send = whole(
        key_kernel,
        smem,
        [cum, v, *key_in, *carried],
        [half] * 2,
        [hold_states],
        after=[started],
        heavy=29,
    )
    key_other = swapped(key_send)
    near = model // plane // 2
    pieces = [shape((SPAN, near, 4 * HEAD))] * SPAN
    hold_rows = pltpu.VMEM((plane, near, 4 * HEAD), BF16)
    (mine,) = whole(
        mine_kernel, (place,), [ring_3], [shape((model // 2, PAIR))], after=[key_send]
    )
    ring_4 = step(mine)

    def one_way(parts):
        moved = [apart(parts[n], ("y", "x"), [(0, n), (n, 0)]) for n in range(1, SPAN)]
        return [parts[0], *moved]

    def other_way(parts):
        moved = [apart(parts[n], ("y", "x"), [(n, 0), (0, n)]) for n in range(1, SPAN)]
        return [parts[0], *moved]

    def halfway(parts):
        return whole(
            halfway_kernel,
            (place,),
            parts,
            [shape((near, 4 * HEAD))] * SPAN,
            [pltpu.VMEM((SPAN, near, 4 * HEAD), BF16)],
        )

    rings = [ring_1, ring_2, ring_3]
    others = [
        swapped(whole(other_kernel, (place,), [r], [shape((model // 2, PAIR))])[0]) for r in rings
    ]
    columns = [own_part]
    for b in bundles:
        columns += [b, swapped(b)]
    parts = whole(
        weight_kernel,
        (place,),
        [own, *rings, *others, ring_4, far_part, swapped(far_part), *columns],
        pieces,
        [hold_rows],
        after=[key_send],
    )
    started = parts[0]
    parts = one_way(parts)
    query_keep, query_send = whole(
        query_kernel,
        smem,
        [cum, g, *query_in, *carried],
        [half] * 2,
        [hold_states],
        after=[started],
        heavy=HEAVY,
    )
    query_other = swapped(query_send)
    (key_grad,) = whole(
        lay_kernel, (place,), [key_keep, key_other], [shape((TOK, width))], after=[started], heavy=HEAVY
    )
    parts = halfway(held(parts, [key_grad]))
    started = parts[0]
    parts = other_way(parts)
    (query_grad,) = whole(
        lay_kernel,
        (place,),
        [query_keep, query_other],
        [shape((TOK, width))],
        after=[started],
        heavy=HEAVY,
    )
    parts = held(parts, [query_grad])
    (weight,) = whole(sum_kernel, (), parts, [shape((near, 4 * HEAD), F32)])
    return query_grad[None], key_grad[None], weight


def solution(mesh):
    fine = Mesh(mesh.devices.reshape(LINE, 4, SPAN, 2), ("z", "y", "x", "core"))
    rows = P("z", CTX, None)
    in_specs = (rows, rows, rows, rows, rows, P("z", None, CTX), P("z", None))
    out_specs = (rows, rows, P(CTX, "z"))
    return jax.shard_map(
        per_device, mesh=fine, in_specs=in_specs, out_specs=out_specs, check_vma=False
    )
```

profile of v0, /device:TPU:34, one launch (start us, length us, event | category | flops | bytes accessed | tf_op | source)
XLA Modules:
  0.0 143.6 jit_solution(15151708048307726393)
XLA Ops:
  0.6 1.1 copy-done.2
  2.3 2.2 %collective-permute-done = bf16[2,16,96,128]{3,2,1,0:T(8,128)(2,1)S(1)} collective-permute-done((bf16[2,16,96,128]{3,2,1,0:T(8,128)(2,1)S(1)}, bf16[2,16,96,128]{3,2,1,0:T(8,128)(2,1)S(1)}, u32[]{:S(2)}, u32[]{:S(2)}) %collective-permute-start) | collective-permute-done | bytes 786464 | tf_op jit(solution)/shard_map/ppermute | solution.py:403
  6.4 1.1 shard_map.96
  7.7 1.9 %collective-permute-start.11 = (bf16[2,1536,256]{2,1,0:T(8,128)(2,1)S(1)}, bf16[2,1536,256]{2,1,0:T(8,128)(2,1)S(1)}, u32[]{:S(2)}, u32[]{:S(2)}) collective-permute-start(bf16[2,1536,256]{2,1,0:T(8,128)(2,1)S(1)} %shard_map.95.refs_6_.refs_1_), channel_id=1, source_target_pairs={{0,32},{1,225},{32,64},{33,1},{64,96},{65,33},{96,128},{97,65},{12... | collective-permute-start | bytes 4718600 | tf_op jit(solution)/shard_map/ppermute | solution.py:422
  9.7 2.1 %collective-permute-done.1.refs_3_ = f32[16,128]{1,0:T(8,128)S(1)} collective-permute-done((f32[16,128]{1,0:T(8,128)S(1)}, f32[16,128]{1,0:T(8,128)S(1)}, u32[]{:S(2)}, u32[]{:S(2)}) %collective-permute-start.1) | collective-permute-done | bytes 8224 | tf_op jit(solution)/shard_map/ppermute | solution.py:403
  11.8 4.5 %shard_map.97 = (bf16[1040,128]{1,0:T(8,128)(2,1)S(1)}, bf16[1040,128]{1,0:T(8,128)(2,1)S(1)}, bf16[1040,128]{1,0:T(8,128)(2,1)S(1)}, bf16[1040,128]{1,0:T(8,128...) custom-call(s32[5]{0:T(128)S(1)} %stack.23.refs_0_, ...), custom_call_target="tpu_custom_call" | custom-call | flops 1 | bytes 1 | tf_op jit(solution)/shard_map/pallas_call | solution.py:366
  16.2 1.6 %collective-permute-start.3 = (bf16[1040,128]{1,0:T(8,128)(2,1)S(1)}, bf16[1040,128]{1,0:T(8,128)(2,1)S(1)}, u32[]{:S(2)}, u32[]{:S(2)}) collective-permute-start(bf16[1040,128]{1,0:T(8,128)(2,1)S(1)} %get-tuple-element.75), channel_id=1, source_target_pairs={{0,2},{2,4},{4,6},{6,0},{1,3},{3,5},{5,7},{7,1},{8,10},{10,12},{12... | collective-permute-start | bytes 798728 | tf_op jit(solution)/shard_map/ppermute | solution.py:403
  17.8 1.1 collective-permute-start.4
  18.9 2.2 %collective-permute-start.5 = (bf16[1040,128]{1,0:T(8,128)(2,1)S(1)}, bf16[1040,128]{1,0:T(8,128)(2,1)S(1)}, u32[]{:S(2)}, u32[]{:S(2)}) collective-permute-start(bf16[1040,128]{1,0:T(8,128)(2,1)S(1)} %get-tuple-element.77), channel_id=1, source_target_pairs={{0,6},{2,0},{4,2},{6,4},{1,7},{3,1},{5,3},{7,5},{8,14},{10,8},{12,... | collective-permute-start | bytes 798728 | tf_op jit(solution)/shard_map/ppermute | solution.py:403
  21.1 7.0 %shard_map.98 = (f32[256,1536]{1,0:T(8,128)S(1)}, f32[256,1536]{1,0:T(8,128)S(1)}, f32[256,1536]{1,0:T(8,128)S(1)}) custom-call(s32[5]{0:T(128)S(1)} %stack.23.refs_0_, s32[4]{0:T(128)S(1)} %bitcast.22, f32[8,2,256]{2,1,0:T(2,128)S(1)} %get-tuple-element.68.refs_2_, bf16[256,2048]{1,0:T(8,128)(2,1)S(1)} %get-tuple-element.70.refs_3_, ...), custom_call_target="tpu_custom_call" | custom-call | flops 4294967296 | bytes 1 | tf_op jit(solution)/shard_map/pallas_call | solution.py:387
  28.6 3.9 %collective-permute-done.5.refs_3_ = bf16[1040,128]{1,0:T(8,128)(2,1)S(1)} collective-permute-done((bf16[1040,128]{1,0:T(8,128)(2,1)S(1)}, bf16[1040,128]{1,0:T(8,128)(2,1)S(1)}, u32[]{:S(2)}, u32[]{:S(2)}) %collective-permute-start.5) | collective-permute-done | bytes 266272 | tf_op jit(solution)/shard_map/ppermute | solution.py:403
  32.5 1.9 %collective-permute-start.12 = (bf16[2,1536,256]{2,1,0:T(8,128)(2,1)S(1)}, bf16[2,1536,256]{2,1,0:T(8,128)(2,1)S(1)}, u32[]{:S(2)}, u32[]{:S(2)}) collective-permute-start(bf16[2,1536,256]{2,1,0:T(8,128)(2,1)S(1)} %shard_map.103.refs_1_.refs_2_), channel_id=1, source_target_pairs={{0,32},{1,225},{32,64},{33,1},{64,96},{65,33},{96,128},{97,65},{12... | collective-permute-start | bytes 4718600 | tf_op jit(solution)/shard_map/ppermute | solution.py:422
  34.4 0.9 shard_map.100
  35.3 1.3 collective-permute-start.6
  36.6 4.6 %collective-permute-start.7 = (bf16[512,128]{1,0:T(8,128)(2,1)S(1)}, bf16[512,128]{1,0:T(8,128)(2,1)S(1)}, u32[]{:S(2)}, u32[]{:S(2)}) collective-permute-start(bf16[512,128]{1,0:T(8,128)(2,1)S(1)} %get-tuple-element.84), channel_id=1, source_target_pairs={{0,8},{8,16},{16,24},{1,9},{9,17},{17,25},{2,10},{10,18},{18,26},{... | collective-permute-start | bytes 393224 | tf_op jit(solution)/shard_map/ppermute | solution.py:473
  41.1 1.6 %collective-permute-done.6.refs_2_ = bf16[512,128]{1,0:T(8,128)(2,1)S(1)} collective-permute-done((bf16[512,128]{1,0:T(8,128)(2,1)S(1)}, bf16[512,128]{1,0:T(8,128)(2,1)S(1)}, u32[]{:S(2)}, u32[]{:S(2)}) %collective-permute-start.6) | collective-permute-done | bytes 131104 | tf_op jit(solution)/shard_map/ppermute | solution.py:472
  42.7 1.2 collective-permute-done.7.refs_3_
  43.9 0.9 shard_map.101
  44.8 1.2 collective-permute-start.10
  46.0 0.9 collective-permute-start.8
  46.9 3.7 %collective-permute-start.9 = (bf16[1024,128]{1,0:T(8,128)(2,1)S(1)}, bf16[1024,128]{1,0:T(8,128)(2,1)S(1)}, u32[]{:S(2)}, u32[]{:S(2)}) collective-permute-start(bf16[1024,128]{1,0:T(8,128)(2,1)S(1)} %get-tuple-element.88), channel_id=1, source_target_pairs={{0,4},{2,6},{4,0},{6,2},{1,5},{3,7},{5,1},{7,3},{8,12},{10,14},{12... | collective-permute-start | bytes 786440 | tf_op jit(solution)/shard_map/ppermute | solution.py:403
  50.7 2.7 %shard_map.102 = (f32[256,512]{1,0:T(8,128)S(1)}, f32[256,512]{1,0:T(8,128)S(1)}, f32[256,512]{1,0:T(8,128)S(1)}) custom-call(s32[5]{0:T(128)S(1)} %stack.23.refs_0_, s32[4]{0:T(128)S(1)} %bitcast.23, f32[8,2,256]{2,1,0:T(2,128)S(1)} %get-tuple-element.68.refs_2_, bf16[256,2048]{1,0:T(8,128)(2,1)S(1)} %get-tuple-element.70.refs_3_, ...), custom_call_target="tpu_custom_call" | custom-call | flops 2147483648 | bytes 1 | tf_op jit(solution)/shard_map/pallas_call | solution.py:387
  53.9 0.9 collective-permute-start.13
  55.8 3.6 %collective-permute-done.9.refs_2_ = bf16[1024,128]{1,0:T(8,128)(2,1)S(1)} collective-permute-done((bf16[1024,128]{1,0:T(8,128)(2,1)S(1)}, bf16[1024,128]{1,0:T(8,128)(2,1)S(1)}, u32[]{:S(2)}, u32[]{:S(2)}) %collective-permute-start.9) | collective-permute-done | bytes 262176 | tf_op jit(solution)/shard_map/ppermute | solution.py:403
  59.3 1.5 %shard_map.109 = (bf16[4,256,256]{2,1,0:T(8,128)(2,1)S(1)}, bf16[5,256,256]{2,1,0:T(8,128)(2,1)S(1)}) custom-call(s32[5]{0:T(128)S(1)} %stack.23.refs_0_, s32[4]{0:T(128)S(1)} %bitcast.24, f32[8,2,256]{2,1,0:T(2,128)S(1)} %get-tuple-element.68.refs_2_, bf16[256,2048]{1,0:T(8,128)(2,1)S(1)} %get-tuple-element.71.refs_4_.refs_3_, ...), custom_call_target="tpu_custom_call" | custom-call | flops 8589934592 | bytes 1 | tf_op jit(solution)/shard_map/pallas_call | solution.py:366
  63.1 4.2 %collective-permute-start.19 = (bf16[256,256]{1,0:T(8,128)(2,1)S(1)}, bf16[256,256]{1,0:T(8,128)(2,1)S(1)}, u32[]{:S(2)}, u32[]{:S(2)}) collective-permute-start(bf16[256,256]{1,0:T(8,128)(2,1)S(1)} %get-tuple-element.102), channel_id=1, source_target_pairs={{0,128},{1,129},{32,160},{33,161},{64,192},{65,193},{96,224},{97,2... | collective-permute-start | bytes 393224 | tf_op jit(solution)/shard_map/ppermute | solution.py:422
  67.2 1.5 %shard_map.111 = (bf16[128,2048]{1,0:T(8,128)(2,1)S(1)}, bf16[128,2048]{1,0:T(8,128)(2,1)S(1)}) custom-call(s32[5]{0:T(128)S(1)} %stack.23.refs_0_, s32[4]{0:T(128)S(1)} %bitcast.25, f32[8,2,256]{2,1,0:T(2,128)S(1)} %get-tuple-element.68.refs_2_, bf16[256,2048]{1,0:T(8,128)(2,1)S(1)} %get-tuple-element.72.refs_5_.refs_3_, ...), custom_call_target="tpu_custom_call" | custom-call | flops 536870912 | bytes 1 | tf_op jit(solution)/shard_map/pallas_call | solution.py:366
  68.7 9.6 %collective-permute-done.13.refs_1_.refs_4_ = bf16[2,1536,256]{2,1,0:T(8,128)(2,1)S(1)} collective-permute-done((bf16[2,1536,256]{2,1,0:T(8,128)(2,1)S(1)}, bf16[2,1536,256]{2,1,0:T(8,128)(2,1)S(1)}, u32[]{:S(2)}, u32[]{:S(2)}) %collective-permute-start.13) | collective-permute-done | bytes 1572896 | tf_op jit(solution)/shard_map/ppermute | solution.py:422
  79.8 6.6 %collective-permute-start.23 = (bf16[2,256,256]{2,1,0:T(8,128)(2,1)S(1)}, bf16[2,256,256]{2,1,0:T(8,128)(2,1)S(1)}, u32[]{:S(2)}, u32[]{:S(2)}) collective-permute-start(bf16[2,256,256]{2,1,0:T(8,128)(2,1)S(1)} %get-tuple-element.104), channel_id=1, source_target_pairs={{0,64},{1,193},{32,96},{33,225},{64,128},{65,1},{96,160},{97,33},{... | collective-permute-start | bytes 786440 | tf_op jit(solution)/shard_map/ppermute | solution.py:422
  86.4 4.0 %collective-permute-start.25 = (bf16[2,256,256]{2,1,0:T(8,128)(2,1)S(1)}, bf16[2,256,256]{2,1,0:T(8,128)(2,1)S(1)}, u32[]{:S(2)}, u32[]{:S(2)}) collective-permute-start(bf16[2,256,256]{2,1,0:T(8,128)(2,1)S(1)} %get-tuple-element.105), channel_id=1, source_target_pairs={{0,96},{1,161},{32,128},{33,193},{64,160},{65,225},{96,192},{97,1}... | collective-permute-start | bytes 786440 | tf_op jit(solution)/shard_map/ppermute | solution.py:422
  90.5 11.9 %collective-permute-done.23.refs_14_ = bf16[2,256,256]{2,1,0:T(8,128)(2,1)S(1)} collective-permute-done((bf16[2,256,256]{2,1,0:T(8,128)(2,1)S(1)}, bf16[2,256,256]{2,1,0:T(8,128)(2,1)S(1)}, u32[]{:S(2)}, u32[]{:S(2)}) %collective-permute-start.23) | collective-permute-done | bytes 262176 | tf_op jit(solution)/shard_map/ppermute | solution.py:422
  102.4 6.8 %collective-permute-done.25.refs_16_ = bf16[2,256,256]{2,1,0:T(8,128)(2,1)S(1)} collective-permute-done((bf16[2,256,256]{2,1,0:T(8,128)(2,1)S(1)}, bf16[2,256,256]{2,1,0:T(8,128)(2,1)S(1)}, u32[]{:S(2)}, u32[]{:S(2)}) %collective-permute-start.25) | collective-permute-done | bytes 262176 | tf_op jit(solution)/shard_map/ppermute | solution.py:422
  109.8 0.9 collective-permute-done.22.refs_13_
  111.5 4.1 %shard_map.113 = (bf16[4,96,512]{2,1,0:T(8,128)(2,1)S(1)}, bf16[4,96,512]{2,1,0:T(8,128)(2,1)S(1)}, bf16[4,96,512]{2,1,0:T(8,128)(2,1)S(1)}, bf16[4,96,512]{2,1,0:T(8,128)(2,1)S(1)}) custom-call(s32[5]{0:T(128)S(1)} %stack.23.refs_0_, bf16[2,1536,256]{2,1,0:T(8,128)(2,1)S(1)} %shard_map.95.refs_6_.refs_1_, ...), custom_call_target="tpu_custom_call" | custom-call | flops 1 | bytes 1 | tf_op jit(solution)/shard_map/pallas_call | solution.py:366
  115.6 1.4 collective-permute-start.28
  117.0 1.6 %collective-permute-start.29 = (bf16[4,96,512]{2,1,0:T(8,128)(2,1)S(1)}, bf16[4,96,512]{2,1,0:T(8,128)(2,1)S(1)}, u32[]{:S(2)}, u32[]{:S(2)}) collective-permute-start(bf16[4,96,512]{2,1,0:T(8,128)(2,1)S(1)} %get-tuple-element.110), channel_id=1, source_target_pairs={{0,4},{1,17},{2,6},{3,19},{4,0},{5,21},{6,2},{7,23},{8,12},{9,25},... | collective-permute-start | bytes 1179656 | tf_op jit(solution)/shard_map/ppermute | solution.py:422
  118.5 1.5 %collective-permute-start.30 = (bf16[4,96,512]{2,1,0:T(8,128)(2,1)S(1)}, bf16[4,96,512]{2,1,0:T(8,128)(2,1)S(1)}, u32[]{:S(2)}, u32[]{:S(2)}) collective-permute-start(bf16[4,96,512]{2,1,0:T(8,128)(2,1)S(1)} %get-tuple-element.111), channel_id=1, source_target_pairs={{0,6},{1,25},{2,0},{3,27},{4,2},{5,29},{6,4},{7,31},{8,14},{9,1},{... | collective-permute-start | bytes 1179656 | tf_op jit(solution)/shard_map/ppermute | solution.py:422
  120.1 1.5 %shard_map.114 = (bf16[128,2048]{1,0:T(8,128)(2,1)S(1)}, bf16[128,2048]{1,0:T(8,128)(2,1)S(1)}) custom-call(s32[5]{0:T(128)S(1)} %stack.23.refs_0_, s32[4]{0:T(128)S(1)} %bitcast.26, f32[8,2,256]{2,1,0:T(2,128)S(1)} %get-tuple-element.68.refs_2_, bf16[256,2048]{1,0:T(8,128)(2,1)S(1)} %get-tuple-element.69.refs_6_.refs_3_, ...), custom_call_target="tpu_custom_call" | custom-call | flops 8589934592 | bytes 1 | tf_op jit(solution)/shard_map/pallas_call | solution.py:366
  122.4 1.6 %shard_map.115.refs_4_ = bf16[128,4096]{1,0:T(8,128)(2,1)} custom-call(s32[5]{0:T(128)S(1)} %stack.23.refs_0_, bf16[128,2048]{1,0:T(8,128)(2,1)S(1)} %get-tuple-element.112.refs_1_, bf16[128,2048]{1,0:T(8,128)(2,1)S(1)} %collective-permute-done.31.refs_2_, bf16[4,96,512]{2,1,0:T(8,128)(2,1)S(1)} %get-tuple-element.106.refs_10_.refs_3_.refs_0_), custom_call_target="tpu_custom_call" | custom-call | flops 8589934592 | bytes 1 | tf_op jit(solution)/shard_map/pallas_call | solution.py:366
  124.0 2.3 %collective-permute-done.29.refs_2_ = bf16[4,96,512]{2,1,0:T(8,128)(2,1)S(1)} collective-permute-done((bf16[4,96,512]{2,1,0:T(8,128)(2,1)S(1)}, bf16[4,96,512]{2,1,0:T(8,128)(2,1)S(1)}, u32[]{:S(2)}, u32[]{:S(2)}) %collective-permute-start.29) | collective-permute-done | bytes 393248 | tf_op jit(solution)/shard_map/ppermute | solution.py:422
  126.3 4.1 %collective-permute-done.30.refs_3_ = bf16[4,96,512]{2,1,0:T(8,128)(2,1)S(1)} collective-permute-done((bf16[4,96,512]{2,1,0:T(8,128)(2,1)S(1)}, bf16[4,96,512]{2,1,0:T(8,128)(2,1)S(1)}, u32[]{:S(2)}, u32[]{:S(2)}) %collective-permute-start.30) | collective-permute-done | bytes 393248 | tf_op jit(solution)/shard_map/ppermute | solution.py:422
  130.4 1.2 copy-done
  132.5 1.7 %collective-permute-start.32 = (bf16[96,512]{1,0:T(8,128)(2,1)S(1)}, bf16[96,512]{1,0:T(8,128)(2,1)S(1)}, u32[]{:S(2)}, u32[]{:S(2)}) collective-permute-start(bf16[96,512]{1,0:T(8,128)(2,1)S(1)} %get-tuple-element.118), channel_id=1, source_target_pairs={{0,8},{1,3},{2,10},{3,5},{4,12},{5,7},{6,14},{7,1},{8,16},{9,11},{... | collective-permute-start | bytes 294920 | tf_op jit(solution)/shard_map/ppermute | solution.py:422
  134.2 2.9 %collective-permute-start.33 = (bf16[96,512]{1,0:T(8,128)(2,1)S(1)}, bf16[96,512]{1,0:T(8,128)(2,1)S(1)}, u32[]{:S(2)}, u32[]{:S(2)}) collective-permute-start(bf16[96,512]{1,0:T(8,128)(2,1)S(1)} %get-tuple-element.119), channel_id=1, source_target_pairs={{0,16},{1,5},{2,18},{3,7},{4,20},{5,1},{6,22},{7,3},{8,24},{9,13},... | collective-permute-start | bytes 294920 | tf_op jit(solution)/shard_map/ppermute | solution.py:422
  137.1 1.3 collective-permute-start.34
  138.4 1.6 %shard_map.118.refs_4_ = bf16[128,4096]{1,0:T(8,128)(2,1)} custom-call(s32[5]{0:T(128)S(1)} %stack.23.refs_0_, bf16[128,2048]{1,0:T(8,128)(2,1)S(1)} %get-tuple-element.107.refs_1_, bf16[128,2048]{1,0:T(8,128)(2,1)S(1)} %collective-permute-done.27.refs_2_, bf16[96,512]{1,0:T(8,128)(2,1)S(1)} %get-tuple-element.117.refs_3_.refs_0_), custom_call_target="tpu_custom_call" | custom-call | flops 8589934592 | bytes 1 | tf_op jit(solution)/shard_map/pallas_call | solution.py:366
  140.7 1.0 collective-permute-done.34.refs_3_
  141.7 1.2 copy-done.1
  (68 shorter events, 12.5 us)
Async XLA Ops:
  0.6 1.1 copy-start.2
  1.8 3.6 %copy-start.7 = (bf16[1,128,4096]{2,1,0:T(8,128)(2,1)S(1)}, bf16[1,128,4096]{2,1,0:T(8,128)(2,1)}, u32[]{:S(2)}) copy-start(bf16[1,128,4096]{2,1,0:T(8,128)(2,1)} %param.10) | copy-start | bytes 3145732
  1.8 3.6 %copy-start.8 = (f32[1,32,128]{2,1,0:T(8,128)S(1)}, f32[1,32,128]{2,1,0:T(8,128)}, u32[]{:S(2)}) copy-start(f32[1,32,128]{2,1,0:T(8,128)} %param.12) | copy-start | bytes 49156
  2.1 2.4 %collective-permute-start = (bf16[2,16,96,128]{3,2,1,0:T(8,128)(2,1)S(1)}, bf16[2,16,96,128]{3,2,1,0:T(8,128)(2,1)S(1)}, u32[]{:S(2)}, u32[]{:S(2)}) collective-permute-start(bf16[2,16,96,128]{3,2,1,0:T(8,128)(2,1)S(1)} %shard_map.94), channel_id=1, source_target_pairs={{0,1},{1,0},{2,3},{3,2},{4,5},{5,4},{6,7},{7,6},{8,9},{9,8},{10,11... | collective-permute-start | bytes 2359304 | tf_op jit(solution)/shard_map/ppermute | solution.py:403
  4.5 1.2 copy-start.4
  4.5 1.5 %copy-start.5 = (bf16[1,128,4096]{2,1,0:T(8,128)(2,1)S(1)}, bf16[1,128,4096]{2,1,0:T(8,128)(2,1)}, u32[]{:S(2)}) copy-start(bf16[1,128,4096]{2,1,0:T(8,128)(2,1)} %param.11) | copy-start | bytes 3145732
  4.5 1.9 %copy-start.6 = (bf16[1,128,4096]{2,1,0:T(8,128)(2,1)S(1)}, bf16[1,128,4096]{2,1,0:T(8,128)(2,1)}, u32[]{:S(2)}) copy-start(bf16[1,128,4096]{2,1,0:T(8,128)(2,1)} %param.9) | copy-start | bytes 3145732
  6.4 5.4 %copy-start.3 = (s32[1,4]{1,0:T(1,128)S(1)}, s32[1,4]{1,0:T(1,128)}, u32[]{:S(2)}) copy-start(s32[1,4]{1,0:T(1,128)} %param.13) | copy-start | bytes 52
  7.5 4.3 %collective-permute-start.2 = (bf16[4,128,2048]{2,1,0:T(8,128)(2,1)S(1)}, bf16[4,128,2048]{2,1,0:T(8,128)(2,1)S(1)}, u32[]{:S(2)}, u32[]{:S(2)}) collective-permute-start(bf16[4,128,2048]{2,1,0:T(8,128)(2,1)S(1)} %get-tuple-element.67), channel_id=1, source_target_pairs={{0,1},{1,0},{2,3},{3,2},{4,5},{5,4},{6,7},{7,6},{8,9},{9,8},{10,11... | collective-permute-start | bytes 6291464 | tf_op jit(solution)/shard_map/ppermute | solution.py:403
  7.7 24.8 %collective-permute-start.11 = (bf16[2,1536,256]{2,1,0:T(8,128)(2,1)S(1)}, bf16[2,1536,256]{2,1,0:T(8,128)(2,1)S(1)}, u32[]{:S(2)}, u32[]{:S(2)}) collective-permute-start(bf16[2,1536,256]{2,1,0:T(8,128)(2,1)S(1)} %shard_map.95.refs_6_.refs_1_), channel_id=1, source_target_pairs={{0,32},{1,225},{32,64},{33,1},{64,96},{65,33},{96,128},{97,65},{12... | collective-permute-start | bytes 4718600 | tf_op jit(solution)/shard_map/ppermute | solution.py:422
  9.7 2.1 %collective-permute-start.1 = (f32[16,128]{1,0:T(8,128)S(1)}, f32[16,128]{1,0:T(8,128)S(1)}, u32[]{:S(2)}, u32[]{:S(2)}) collective-permute-start(f32[16,128]{1,0:T(8,128)S(1)} %get-tuple-element.65), channel_id=1, source_target_pairs={{0,1},{1,0},{2,3},{3,2},{4,5},{5,4},{6,7},{7,6},{8,9},{9,8},{10,11... | collective-permute-start | bytes 24584 | tf_op jit(solution)/shard_map/ppermute | solution.py:403
  16.2 11.9 %collective-permute-start.3 = (bf16[1040,128]{1,0:T(8,128)(2,1)S(1)}, bf16[1040,128]{1,0:T(8,128)(2,1)S(1)}, u32[]{:S(2)}, u32[]{:S(2)}) collective-permute-start(bf16[1040,128]{1,0:T(8,128)(2,1)S(1)} %get-tuple-element.75), channel_id=1, source_target_pairs={{0,2},{2,4},{4,6},{6,0},{1,3},{3,5},{5,7},{7,1},{8,10},{10,12},{12... | collective-permute-start | bytes 798728 | tf_op jit(solution)/shard_map/ppermute | solution.py:403
  17.8 10.8 %collective-permute-start.4 = (bf16[1040,128]{1,0:T(8,128)(2,1)S(1)}, bf16[1040,128]{1,0:T(8,128)(2,1)S(1)}, u32[]{:S(2)}, u32[]{:S(2)}) collective-permute-start(bf16[1040,128]{1,0:T(8,128)(2,1)S(1)} %get-tuple-element.76), channel_id=1, source_target_pairs={{0,4},{2,6},{4,0},{6,2},{1,5},{3,7},{5,1},{7,3},{8,12},{10,14},{12... | collective-permute-start | bytes 798728 | tf_op jit(solution)/shard_map/ppermute | solution.py:403
  18.9 13.6 %collective-permute-start.5 = (bf16[1040,128]{1,0:T(8,128)(2,1)S(1)}, bf16[1040,128]{1,0:T(8,128)(2,1)S(1)}, u32[]{:S(2)}, u32[]{:S(2)}) collective-permute-start(bf16[1040,128]{1,0:T(8,128)(2,1)S(1)} %get-tuple-element.77), channel_id=1, source_target_pairs={{0,6},{2,0},{4,2},{6,4},{1,7},{3,1},{5,3},{7,5},{8,14},{10,8},{12,... | collective-permute-start | bytes 798728 | tf_op jit(solution)/shard_map/ppermute | solution.py:403
  32.5 21.5 %collective-permute-start.12 = (bf16[2,1536,256]{2,1,0:T(8,128)(2,1)S(1)}, bf16[2,1536,256]{2,1,0:T(8,128)(2,1)S(1)}, u32[]{:S(2)}, u32[]{:S(2)}) collective-permute-start(bf16[2,1536,256]{2,1,0:T(8,128)(2,1)S(1)} %shard_map.103.refs_1_.refs_2_), channel_id=1, source_target_pairs={{0,32},{1,225},{32,64},{33,1},{64,96},{65,33},{96,128},{97,65},{12... | collective-permute-start | bytes 4718600 | tf_op jit(solution)/shard_map/ppermute | solution.py:422
  35.3 7.4 %collective-permute-start.6 = (bf16[512,128]{1,0:T(8,128)(2,1)S(1)}, bf16[512,128]{1,0:T(8,128)(2,1)S(1)}, u32[]{:S(2)}, u32[]{:S(2)}) collective-permute-start(bf16[512,128]{1,0:T(8,128)(2,1)S(1)} %get-tuple-element.83), channel_id=1, source_target_pairs={{8,0},{16,8},{24,16},{9,1},{17,9},{25,17},{10,2},{18,10},{26,18},{... | collective-permute-start | bytes 393224 | tf_op jit(solution)/shard_map/ppermute | solution.py:472
  36.6 7.3 %collective-permute-start.7 = (bf16[512,128]{1,0:T(8,128)(2,1)S(1)}, bf16[512,128]{1,0:T(8,128)(2,1)S(1)}, u32[]{:S(2)}, u32[]{:S(2)}) collective-permute-start(bf16[512,128]{1,0:T(8,128)(2,1)S(1)} %get-tuple-element.84), channel_id=1, source_target_pairs={{0,8},{8,16},{16,24},{1,9},{9,17},{17,25},{2,10},{10,18},{18,26},{... | collective-permute-start | bytes 393224 | tf_op jit(solution)/shard_map/ppermute | solution.py:473
  44.8 10.7 %collective-permute-start.10 = (bf16[1024,128]{1,0:T(8,128)(2,1)S(1)}, bf16[1024,128]{1,0:T(8,128)(2,1)S(1)}, u32[]{:S(2)}, u32[]{:S(2)}) collective-permute-start(bf16[1024,128]{1,0:T(8,128)(2,1)S(1)} %get-tuple-element.89), channel_id=1, source_target_pairs={{0,6},{2,0},{4,2},{6,4},{1,7},{3,1},{5,3},{7,5},{8,14},{10,8},{12,... | collective-permute-start | bytes 786440 | tf_op jit(solution)/shard_map/ppermute | solution.py:403
  46.0 9.7 %collective-permute-start.8 = (bf16[1024,128]{1,0:T(8,128)(2,1)S(1)}, bf16[1024,128]{1,0:T(8,128)(2,1)S(1)}, u32[]{:S(2)}, u32[]{:S(2)}) collective-permute-start(bf16[1024,128]{1,0:T(8,128)(2,1)S(1)} %get-tuple-element.87), channel_id=1, source_target_pairs={{0,2},{2,4},{4,6},{6,0},{1,3},{3,5},{5,7},{7,1},{8,10},{10,12},{12... | collective-permute-start | bytes 786440 | tf_op jit(solution)/shard_map/ppermute | solution.py:403
  46.9 12.4 %collective-permute-start.9 = (bf16[1024,128]{1,0:T(8,128)(2,1)S(1)}, bf16[1024,128]{1,0:T(8,128)(2,1)S(1)}, u32[]{:S(2)}, u32[]{:S(2)}) collective-permute-start(bf16[1024,128]{1,0:T(8,128)(2,1)S(1)} %get-tuple-element.88), channel_id=1, source_target_pairs={{0,4},{2,6},{4,0},{6,2},{1,5},{3,7},{5,1},{7,3},{8,12},{10,14},{12... | collective-permute-start | bytes 786440 | tf_op jit(solution)/shard_map/ppermute | solution.py:403
  53.9 24.4 %collective-permute-start.13 = (bf16[2,1536,256]{2,1,0:T(8,128)(2,1)S(1)}, bf16[2,1536,256]{2,1,0:T(8,128)(2,1)S(1)}, u32[]{:S(2)}, u32[]{:S(2)}) collective-permute-start(bf16[2,1536,256]{2,1,0:T(8,128)(2,1)S(1)} %shard_map.104.refs_4_.refs_1_.refs_3_), channel_id=1, source_target_pairs={{0,32},{1,225},{32,64},{33,1},{64,96},{65,33},{96,128},{97,65},{12... | collective-permute-start | bytes 4718600 | tf_op jit(solution)/shard_map/ppermute | solution.py:422
  55.4 24.3 %collective-permute-start.14 = (bf16[1536,256]{1,0:T(8,128)(2,1)S(1)}, bf16[1536,256]{1,0:T(8,128)(2,1)S(1)}, u32[]{:S(2)}, u32[]{:S(2)}) collective-permute-start(bf16[1536,256]{1,0:T(8,128)(2,1)S(1)} %shard_map.106), channel_id=1, source_target_pairs={{0,1},{1,0},{2,3},{3,2},{4,5},{5,4},{6,7},{7,6},{8,9},{9,8},{10,11... | collective-permute-start | bytes 2359304 | tf_op jit(solution)/shard_map/ppermute | solution.py:403
  60.9 2.0 %collective-permute-start.17 = (bf16[4,256,256]{2,1,0:T(8,128)(2,1)S(1)}, bf16[4,256,256]{2,1,0:T(8,128)(2,1)S(1)}, u32[]{:S(2)}, u32[]{:S(2)}) collective-permute-start(bf16[4,256,256]{2,1,0:T(8,128)(2,1)S(1)} %get-tuple-element.99), channel_id=1, source_target_pairs={{0,1},{1,0},{2,3},{3,2},{4,5},{5,4},{6,7},{7,6},{8,9},{9,8},{10,11... | collective-permute-start | bytes 1572872 | tf_op jit(solution)/shard_map/ppermute | solution.py:403
  61.6 48.1 %collective-permute-start.15 = (bf16[1536,256]{1,0:T(8,128)(2,1)S(1)}, bf16[1536,256]{1,0:T(8,128)(2,1)S(1)}, u32[]{:S(2)}, u32[]{:S(2)}) collective-permute-start(bf16[1536,256]{1,0:T(8,128)(2,1)S(1)} %shard_map.107), channel_id=1, source_target_pairs={{0,1},{1,0},{2,3},{3,2},{4,5},{5,4},{6,7},{7,6},{8,9},{9,8},{10,11... | collective-permute-start | bytes 2359304 | tf_op jit(solution)/shard_map/ppermute | solution.py:403
  63.0 23.5 %collective-permute-start.21 = (bf16[2,256,256]{2,1,0:T(8,128)(2,1)S(1)}, bf16[2,256,256]{2,1,0:T(8,128)(2,1)S(1)}, u32[]{:S(2)}, u32[]{:S(2)}) collective-permute-start(bf16[2,256,256]{2,1,0:T(8,128)(2,1)S(1)} %get-tuple-element.100.refs_10_), channel_id=1, source_target_pairs={{0,32},{1,225},{32,64},{33,1},{64,96},{65,33},{96,128},{97,65},{12... | collective-permute-start | bytes 786440 | tf_op jit(solution)/shard_map/ppermute | solution.py:422
  63.1 16.7 %collective-permute-start.19 = (bf16[256,256]{1,0:T(8,128)(2,1)S(1)}, bf16[256,256]{1,0:T(8,128)(2,1)S(1)}, u32[]{:S(2)}, u32[]{:S(2)}) collective-permute-start(bf16[256,256]{1,0:T(8,128)(2,1)S(1)} %get-tuple-element.102), channel_id=1, source_target_pairs={{0,128},{1,129},{32,160},{33,161},{64,192},{65,193},{96,224},{97,2... | collective-permute-start | bytes 393224 | tf_op jit(solution)/shard_map/ppermute | solution.py:422
  79.0 32.5 %collective-permute-start.18 = (bf16[1536,256]{1,0:T(8,128)(2,1)S(1)}, bf16[1536,256]{1,0:T(8,128)(2,1)S(1)}, u32[]{:S(2)}, u32[]{:S(2)}) collective-permute-start(bf16[1536,256]{1,0:T(8,128)(2,1)S(1)} %shard_map.112), channel_id=1, source_target_pairs={{0,32},{1,225},{32,64},{33,1},{64,96},{65,33},{96,128},{97,65},{12... | collective-permute-start | bytes 2359304 | tf_op jit(solution)/shard_map/ppermute | solution.py:422
  79.7 31.8 %collective-permute-start.16 = (bf16[1536,256]{1,0:T(8,128)(2,1)S(1)}, bf16[1536,256]{1,0:T(8,128)(2,1)S(1)}, u32[]{:S(2)}, u32[]{:S(2)}) collective-permute-start(bf16[1536,256]{1,0:T(8,128)(2,1)S(1)} %shard_map.108), channel_id=1, source_target_pairs={{0,1},{1,0},{2,3},{3,2},{4,5},{5,4},{6,7},{7,6},{8,9},{9,8},{10,11... | collective-permute-start | bytes 2359304 | tf_op jit(solution)/shard_map/ppermute | solution.py:403
  79.8 22.6 %collective-permute-start.23 = (bf16[2,256,256]{2,1,0:T(8,128)(2,1)S(1)}, bf16[2,256,256]{2,1,0:T(8,128)(2,1)S(1)}, u32[]{:S(2)}, u32[]{:S(2)}) collective-permute-start(bf16[2,256,256]{2,1,0:T(8,128)(2,1)S(1)} %get-tuple-element.104), channel_id=1, source_target_pairs={{0,64},{1,193},{32,96},{33,225},{64,128},{65,1},{96,160},{97,33},{... | collective-permute-start | bytes 786440 | tf_op jit(solution)/shard_map/ppermute | solution.py:422
  86.4 22.7 %collective-permute-start.25 = (bf16[2,256,256]{2,1,0:T(8,128)(2,1)S(1)}, bf16[2,256,256]{2,1,0:T(8,128)(2,1)S(1)}, u32[]{:S(2)}, u32[]{:S(2)}) collective-permute-start(bf16[2,256,256]{2,1,0:T(8,128)(2,1)S(1)} %get-tuple-element.105), channel_id=1, source_target_pairs={{0,96},{1,161},{32,128},{33,193},{64,160},{65,225},{96,192},{97,1}... | collective-permute-start | bytes 786440 | tf_op jit(solution)/shard_map/ppermute | solution.py:422
  102.4 6.8 %collective-permute-start.20 = (bf16[256,256]{1,0:T(8,128)(2,1)S(1)}, bf16[256,256]{1,0:T(8,128)(2,1)S(1)}, u32[]{:S(2)}, u32[]{:S(2)}) collective-permute-start(bf16[256,256]{1,0:T(8,128)(2,1)S(1)} %collective-permute-done.19.refs_9_), channel_id=1, source_target_pairs={{0,1},{1,0},{2,3},{3,2},{4,5},{5,4},{6,7},{7,6},{8,9},{9,8},{10,11... | collective-permute-start | bytes 393224 | tf_op jit(solution)/shard_map/ppermute | solution.py:403
  109.2 1.5 %collective-permute-start.22 = (bf16[2,256,256]{2,1,0:T(8,128)(2,1)S(1)}, bf16[2,256,256]{2,1,0:T(8,128)(2,1)S(1)}, u32[]{:S(2)}, u32[]{:S(2)}) collective-permute-start(bf16[2,256,256]{2,1,0:T(8,128)(2,1)S(1)} %collective-permute-done.21.refs_12_), channel_id=1, source_target_pairs={{0,1},{1,0},{2,3},{3,2},{4,5},{5,4},{6,7},{7,6},{8,9},{9,8},{10,11... | collective-permute-start | bytes 786440 | tf_op jit(solution)/shard_map/ppermute | solution.py:403
  109.2 1.9 %collective-permute-start.24 = (bf16[2,256,256]{2,1,0:T(8,128)(2,1)S(1)}, bf16[2,256,256]{2,1,0:T(8,128)(2,1)S(1)}, u32[]{:S(2)}, u32[]{:S(2)}) collective-permute-start(bf16[2,256,256]{2,1,0:T(8,128)(2,1)S(1)} %collective-permute-done.23.refs_14_), channel_id=1, source_target_pairs={{0,1},{1,0},{2,3},{3,2},{4,5},{5,4},{6,7},{7,6},{8,9},{9,8},{10,11... | collective-permute-start | bytes 786440 | tf_op jit(solution)/shard_map/ppermute | solution.py:403
  109.7 1.8 %collective-permute-start.26 = (bf16[2,256,256]{2,1,0:T(8,128)(2,1)S(1)}, bf16[2,256,256]{2,1,0:T(8,128)(2,1)S(1)}, u32[]{:S(2)}, u32[]{:S(2)}) collective-permute-start(bf16[2,256,256]{2,1,0:T(8,128)(2,1)S(1)} %collective-permute-done.25.refs_16_), channel_id=1, source_target_pairs={{0,1},{1,0},{2,3},{3,2},{4,5},{5,4},{6,7},{7,6},{8,9},{9,8},{10,11... | collective-permute-start | bytes 786440 | tf_op jit(solution)/shard_map/ppermute | solution.py:403
  110.7 11.6 %collective-permute-start.31 = (bf16[128,2048]{1,0:T(8,128)(2,1)S(1)}, bf16[128,2048]{1,0:T(8,128)(2,1)S(1)}, u32[]{:S(2)}, u32[]{:S(2)}) collective-permute-start(bf16[128,2048]{1,0:T(8,128)(2,1)S(1)} %get-tuple-element.101.refs_2_.refs_18_), channel_id=1, source_target_pairs={{0,1},{1,0},{2,3},{3,2},{4,5},{5,4},{6,7},{7,6},{8,9},{9,8},{10,11... | collective-permute-start | bytes 1572872 | tf_op jit(solution)/shard_map/ppermute | solution.py:403
  115.6 8.4 %collective-permute-start.28 = (bf16[4,96,512]{2,1,0:T(8,128)(2,1)S(1)}, bf16[4,96,512]{2,1,0:T(8,128)(2,1)S(1)}, u32[]{:S(2)}, u32[]{:S(2)}) collective-permute-start(bf16[4,96,512]{2,1,0:T(8,128)(2,1)S(1)} %get-tuple-element.109), channel_id=1, source_target_pairs={{0,2},{1,9},{2,4},{3,11},{4,6},{5,13},{6,0},{7,15},{8,10},{9,17},{... | collective-permute-start | bytes 1179656 | tf_op jit(solution)/shard_map/ppermute | solution.py:422
  117.0 9.4 %collective-permute-start.29 = (bf16[4,96,512]{2,1,0:T(8,128)(2,1)S(1)}, bf16[4,96,512]{2,1,0:T(8,128)(2,1)S(1)}, u32[]{:S(2)}, u32[]{:S(2)}) collective-permute-start(bf16[4,96,512]{2,1,0:T(8,128)(2,1)S(1)} %get-tuple-element.110), channel_id=1, source_target_pairs={{0,4},{1,17},{2,6},{3,19},{4,0},{5,21},{6,2},{7,23},{8,12},{9,25},... | collective-permute-start | bytes 1179656 | tf_op jit(solution)/shard_map/ppermute | solution.py:422
  118.5 11.9 %collective-permute-start.30 = (bf16[4,96,512]{2,1,0:T(8,128)(2,1)S(1)}, bf16[4,96,512]{2,1,0:T(8,128)(2,1)S(1)}, u32[]{:S(2)}, u32[]{:S(2)}) collective-permute-start(bf16[4,96,512]{2,1,0:T(8,128)(2,1)S(1)} %get-tuple-element.111), channel_id=1, source_target_pairs={{0,6},{1,25},{2,0},{3,27},{4,2},{5,29},{6,4},{7,31},{8,14},{9,1},{... | collective-permute-start | bytes 1179656 | tf_op jit(solution)/shard_map/ppermute | solution.py:422
  121.5 16.9 %collective-permute-start.27 = (bf16[128,2048]{1,0:T(8,128)(2,1)S(1)}, bf16[128,2048]{1,0:T(8,128)(2,1)S(1)}, u32[]{:S(2)}, u32[]{:S(2)}) collective-permute-start(bf16[128,2048]{1,0:T(8,128)(2,1)S(1)} %get-tuple-element.108), channel_id=1, source_target_pairs={{0,1},{1,0},{2,3},{3,2},{4,5},{5,4},{6,7},{7,6},{8,9},{9,8},{10,11... | collective-permute-start | bytes 1572872 | tf_op jit(solution)/shard_map/ppermute | solution.py:403
  130.4 1.2 copy-start
  132.5 7.5 %collective-permute-start.32 = (bf16[96,512]{1,0:T(8,128)(2,1)S(1)}, bf16[96,512]{1,0:T(8,128)(2,1)S(1)}, u32[]{:S(2)}, u32[]{:S(2)}) collective-permute-start(bf16[96,512]{1,0:T(8,128)(2,1)S(1)} %get-tuple-element.118), channel_id=1, source_target_pairs={{0,8},{1,3},{2,10},{3,5},{4,12},{5,7},{6,14},{7,1},{8,16},{9,11},{... | collective-permute-start | bytes 294920 | tf_op jit(solution)/shard_map/ppermute | solution.py:422
  134.2 6.5 %collective-permute-start.33 = (bf16[96,512]{1,0:T(8,128)(2,1)S(1)}, bf16[96,512]{1,0:T(8,128)(2,1)S(1)}, u32[]{:S(2)}, u32[]{:S(2)}) collective-permute-start(bf16[96,512]{1,0:T(8,128)(2,1)S(1)} %get-tuple-element.119), channel_id=1, source_target_pairs={{0,16},{1,5},{2,18},{3,7},{4,20},{5,1},{6,22},{7,3},{8,24},{9,13},... | collective-permute-start | bytes 294920 | tf_op jit(solution)/shard_map/ppermute | solution.py:422
  137.1 4.6 %collective-permute-start.34 = (bf16[96,512]{1,0:T(8,128)(2,1)S(1)}, bf16[96,512]{1,0:T(8,128)(2,1)S(1)}, u32[]{:S(2)}, u32[]{:S(2)}) collective-permute-start(bf16[96,512]{1,0:T(8,128)(2,1)S(1)} %get-tuple-element.120), channel_id=1, source_target_pairs={{0,24},{1,7},{2,26},{3,1},{4,28},{5,3},{6,30},{7,5},{8,0},{9,15},{... | collective-permute-start | bytes 294920 | tf_op jit(solution)/shard_map/ppermute | solution.py:422
  141.7 1.2 copy-start.1
where the time goes:
time: 144 us
  waiting for transfers between devices  54.5 us (38%)
  starting transfers between devices  49.4 us (34%)
  Pallas kernels  34.1 us (24%)
  local copies, waits for them, and re-layouts  4.69 us (3%)
    ppermute x14, waiting for transfers between devices, apart(): return lax.ppermute(value, (*axes, 'core'), pairs)  37 us
    ppermute x14, starting transfers between devices, apart(): return lax.ppermute(value, (*axes, 'core'), pairs)  30.1 us
    pallas_call x19, Pallas kernels, whole(): pl.pallas_call(body, in_specs=[pl.BlockSpec(memory_space=pltpu.SMEM)] * l...  24.5 us
    ppermute x19, waiting for transfers between devices, shifted(): lax.ppermute(value, axis, [(i, (i + step) % count) for i in range(count)])  14.7 us
    ppermute x19, starting transfers between devices, shifted(): lax.ppermute(value, axis, [(i, (i + step) % count) for i in range(count)])  13.4 us
    pallas_call x2, Pallas kernels, inner(): pl.pallas_call(body, grid=(high - low,), in_specs=[pl.BlockSpec(memory_sp...  9.65 us
    unnamed x18, local copies, waits for them, and re-layouts  4.6 us
    ppermute x1, starting transfers between devices, per_device(): front = lax.ppermute(front, 'y', [(i, i + 1) for i in range(count - 1)])  4.55 us
  transfers between devices with their start and end apart: 35, of which 20 were waited for; matrix products, arithmetic and copies ran while one was open for 0% of the time, Pallas kernels for 22%

commit v1 on v0

--- a/solution.py
+++ b/solution.py
@@ -262,13 +262,13 @@
         part_rows(place_ref[1], piece_of(query_in, h) + extra, head_cut(h), keep_ref, send_ref)
 
 
-def lay_kernel(place_ref, keep_ref, other_ref, out_ref):
-    core = place_ref[1]
-    for d in range(LINE):
-        near = slice(2 * d * HEAD, 2 * (d + 1) * HEAD)
-        for source, who in ((keep_ref, core), (other_ref, 1 - core)):
-            lanes = pl.ds(pl.multiple_of((2 * d + who) * 2 * HEAD, 2 * HEAD), 2 * HEAD)
-            out_ref[:, lanes] = source[:, near]
+def lay_kernel(place_ref, keep_ref, other_ref, *refs):
+    first, out_ref, wide = place_ref[1] == 0, refs[-1], 2 * HEAD
+    for d in range(keep_ref.shape[1] // wide):
+        near = slice(d * wide, (d + 1) * wide)
+        keep, other = keep_ref[:, near], other_ref[:, near]
+        out_ref[:, 2 * d * wide : (2 * d + 1) * wide] = jnp.where(first, keep, other)
+        out_ref[:, (2 * d + 1) * wide : 2 * (d + 1) * wide] = jnp.where(first, other, keep)
 
 
 def by_core(place_ref, keep, other):
@@ -398,6 +398,22 @@
     )(*smem, cum, *arrays, *after)
 
 
+def lay(place, keep, other, after, heavy):
+    steps = 4
+    wide = keep.shape[1] // steps
+    block = pl.BlockSpec((TOK, wide), lambda i: (0, i))
+    return pl.pallas_call(
+        lay_kernel,
+        grid=(steps,),
+        in_specs=[pl.BlockSpec(memory_space=pltpu.SMEM), block, block]
+        + [pl.BlockSpec(memory_space=pl.ANY)] * len(after),
+        out_specs=pl.BlockSpec((TOK, 2 * wide), lambda i: (0, i)),
+        out_shape=shape((TOK, 2 * keep.shape[1])),
+        compiler_params=pltpu.CompilerParams(vmem_limit_bytes=VMEM_LIMIT),
+        cost_estimate=cost(heavy),
+    )(place, keep, other, *after)
+
+
 def shifted(value, axis, step):
     count = lax.axis_size(axis)
     return lax.ppermute(value, axis, [(i, (i + step) % count) for i in range(count)])
@@ -564,20 +580,11 @@
         heavy=HEAVY,
     )
     query_other = swapped(query_send)
-    (key_grad,) = whole(
-        lay_kernel, (place,), [key_keep, key_other], [shape((TOK, width))], after=[started], heavy=HEAVY
-    )
+    key_grad = lay(place, key_keep, key_other, [started], HEAVY)
     parts = halfway(held(parts, [key_grad]))
     started = parts[0]
     parts = other_way(parts)
-    (query_grad,) = whole(
-        lay_kernel,
-        (place,),
-        [query_keep, query_other],
-        [shape((TOK, width))],
-        after=[started],
-        heavy=HEAVY,
-    )
+    query_grad = lay(place, query_keep, query_other, [started], HEAVY)
     parts = held(parts, [query_grad])
     (weight,) = whole(sum_kernel, (), parts, [shape((near, 4 * HEAD), F32)])
     return query_grad[None], key_grad[None], weight

time: 144 us -> 144 us (level)
    pallas_call x0 -> x2, Pallas kernels: none -> 4.31 us  [lay(): pl.pallas_call(lay_kernel, grid=(steps,), in_specs=[pl.BlockSpec(memory_s...]
    pallas_call x19 -> x17, Pallas kernels: 24.5 us -> 21.2 us  [whole(): pl.pallas_call(body, in_specs=[pl.BlockSpec(memory_space=pltpu.SMEM)] * l...]
where the time goes in v1:
time: 144 us
  waiting for transfers between devices  53.5 us (37%)
  starting transfers between devices  49.4 us (34%)
  Pallas kernels  35.2 us (24%)
  local copies, waits for them, and re-layouts  4.69 us (3%)
    ppermute x14, waiting for transfers between devices, apart(): return lax.ppermute(value, (*axes, 'core'), pairs)  36 us
    ppermute x14, starting transfers between devices, apart(): return lax.ppermute(value, (*axes, 'core'), pairs)  30.1 us
    pallas_call x17, Pallas kernels, whole(): pl.pallas_call(body, in_specs=[pl.BlockSpec(memory_space=pltpu.SMEM)] * l...  21.2 us
    ppermute x19, waiting for transfers between devices, shifted(): lax.ppermute(value, axis, [(i, (i + step) % count) for i in range(count)])  14.7 us
    ppermute x19, starting transfers between devices, shifted(): lax.ppermute(value, axis, [(i, (i + step) % count) for i in range(count)])  13.4 us
    pallas_call x2, Pallas kernels, inner(): pl.pallas_call(body, grid=(high - low,), in_specs=[pl.BlockSpec(memory_sp...  9.65 us
    unnamed x18, local copies, waits for them, and re-layouts  4.6 us
    ppermute x1, starting transfers between devices, per_device(): front = lax.ppermute(front, 'y', [(i, i + 1) for i in range(count - 1)])  4.55 us
  transfers between devices with their start and end apart: 35, of which 20 were waited for; matrix products, arithmetic and copies ran while one was open for 0% of the time, Pallas kernels for 22%

profile of v1, /device:TPU:34, one launch (start us, length us, event | category | flops | bytes accessed | tf_op | source)
XLA Modules:
  0.0 143.6 jit_solution(11396173010471356657)
XLA Ops:
  0.6 1.1 copy-done.2
  2.3 2.2 %collective-permute-done = bf16[2,16,96,128]{3,2,1,0:T(8,128)(2,1)S(1)} collective-permute-done((bf16[2,16,96,128]{3,2,1,0:T(8,128)(2,1)S(1)}, bf16[2,16,96,128]{3,2,1,0:T(8,128)(2,1)S(1)}, u32[]{:S(2)}, u32[]{:S(2)}) %collective-permute-start) | collective-permute-done | bytes 786464 | tf_op jit(solution)/shard_map/ppermute | solution.py:419
  6.4 1.1 shard_map.96
  7.7 1.9 %collective-permute-start.11 = (bf16[2,1536,256]{2,1,0:T(8,128)(2,1)S(1)}, bf16[2,1536,256]{2,1,0:T(8,128)(2,1)S(1)}, u32[]{:S(2)}, u32[]{:S(2)}) collective-permute-start(bf16[2,1536,256]{2,1,0:T(8,128)(2,1)S(1)} %shard_map.95.refs_6_.refs_1_), channel_id=1, source_target_pairs={{0,32},{1,225},{32,64},{33,1},{64,96},{65,33},{96,128},{97,65},{12... | collective-permute-start | bytes 4718600 | tf_op jit(solution)/shard_map/ppermute | solution.py:438
  9.7 2.1 %collective-permute-done.1.refs_3_ = f32[16,128]{1,0:T(8,128)S(1)} collective-permute-done((f32[16,128]{1,0:T(8,128)S(1)}, f32[16,128]{1,0:T(8,128)S(1)}, u32[]{:S(2)}, u32[]{:S(2)}) %collective-permute-start.1) | collective-permute-done | bytes 8224 | tf_op jit(solution)/shard_map/ppermute | solution.py:419
  11.8 4.5 %shard_map.97 = (bf16[1040,128]{1,0:T(8,128)(2,1)S(1)}, bf16[1040,128]{1,0:T(8,128)(2,1)S(1)}, bf16[1040,128]{1,0:T(8,128)(2,1)S(1)}, bf16[1040,128]{1,0:T(8,128...) custom-call(s32[5]{0:T(128)S(1)} %stack.23.refs_0_.place_ref, ...), custom_call_target="tpu_custom_call" | custom-call | flops 1 | bytes 1 | tf_op jit(solution)/shard_map/pallas_call | solution.py:366
  16.2 1.6 %collective-permute-start.3 = (bf16[1040,128]{1,0:T(8,128)(2,1)S(1)}, bf16[1040,128]{1,0:T(8,128)(2,1)S(1)}, u32[]{:S(2)}, u32[]{:S(2)}) collective-permute-start(bf16[1040,128]{1,0:T(8,128)(2,1)S(1)} %get-tuple-element.75), channel_id=1, source_target_pairs={{0,2},{2,4},{4,6},{6,0},{1,3},{3,5},{5,7},{7,1},{8,10},{10,12},{12... | collective-permute-start | bytes 798728 | tf_op jit(solution)/shard_map/ppermute | solution.py:419
  17.8 1.1 collective-permute-start.4
  18.9 2.2 %collective-permute-start.5 = (bf16[1040,128]{1,0:T(8,128)(2,1)S(1)}, bf16[1040,128]{1,0:T(8,128)(2,1)S(1)}, u32[]{:S(2)}, u32[]{:S(2)}) collective-permute-start(bf16[1040,128]{1,0:T(8,128)(2,1)S(1)} %get-tuple-element.77), channel_id=1, source_target_pairs={{0,6},{2,0},{4,2},{6,4},{1,7},{3,1},{5,3},{7,5},{8,14},{10,8},{12,... | collective-permute-start | bytes 798728 | tf_op jit(solution)/shard_map/ppermute | solution.py:419
  21.1 7.0 %shard_map.98 = (f32[256,1536]{1,0:T(8,128)S(1)}, f32[256,1536]{1,0:T(8,128)S(1)}, f32[256,1536]{1,0:T(8,128)S(1)}) custom-call(s32[5]{0:T(128)S(1)} %stack.23.refs_0_.place_ref, s32[4]{0:T(128)S(1)} %bitcast.22, f32[8,2,256]{2,1,0:T(2,128)S(1)} %get-tuple-element.68.refs_2_, bf16[256,2048]{1,0:T(8,128)(2,1)S(1)} %get-tuple-element.70.refs_3_, ...), custom_call_target="tpu_custom_call" | custom-call | flops 4294967296 | bytes 1 | tf_op jit(solution)/shard_map/pallas_call | solution.py:387
  28.6 3.9 %collective-permute-done.5.refs_3_ = bf16[1040,128]{1,0:T(8,128)(2,1)S(1)} collective-permute-done((bf16[1040,128]{1,0:T(8,128)(2,1)S(1)}, bf16[1040,128]{1,0:T(8,128)(2,1)S(1)}, u32[]{:S(2)}, u32[]{:S(2)}) %collective-permute-start.5) | collective-permute-done | bytes 266272 | tf_op jit(solution)/shard_map/ppermute | solution.py:419
  32.5 1.9 %collective-permute-start.12 = (bf16[2,1536,256]{2,1,0:T(8,128)(2,1)S(1)}, bf16[2,1536,256]{2,1,0:T(8,128)(2,1)S(1)}, u32[]{:S(2)}, u32[]{:S(2)}) collective-permute-start(bf16[2,1536,256]{2,1,0:T(8,128)(2,1)S(1)} %shard_map.103.refs_1_.refs_2_), channel_id=1, source_target_pairs={{0,32},{1,225},{32,64},{33,1},{64,96},{65,33},{96,128},{97,65},{12... | collective-permute-start | bytes 4718600 | tf_op jit(solution)/shard_map/ppermute | solution.py:438
  34.4 0.9 shard_map.100
  35.3 1.3 collective-permute-start.6
  36.6 4.6 %collective-permute-start.7 = (bf16[512,128]{1,0:T(8,128)(2,1)S(1)}, bf16[512,128]{1,0:T(8,128)(2,1)S(1)}, u32[]{:S(2)}, u32[]{:S(2)}) collective-permute-start(bf16[512,128]{1,0:T(8,128)(2,1)S(1)} %get-tuple-element.84), channel_id=1, source_target_pairs={{0,8},{8,16},{16,24},{1,9},{9,17},{17,25},{2,10},{10,18},{18,26},{... | collective-permute-start | bytes 393224 | tf_op jit(solution)/shard_map/ppermute | solution.py:489
  41.1 1.6 %collective-permute-done.6.refs_2_ = bf16[512,128]{1,0:T(8,128)(2,1)S(1)} collective-permute-done((bf16[512,128]{1,0:T(8,128)(2,1)S(1)}, bf16[512,128]{1,0:T(8,128)(2,1)S(1)}, u32[]{:S(2)}, u32[]{:S(2)}) %collective-permute-start.6) | collective-permute-done | bytes 131104 | tf_op jit(solution)/shard_map/ppermute | solution.py:488
  42.7 1.2 collective-permute-done.7.refs_3_
  43.9 0.9 shard_map.101
  44.8 1.2 collective-permute-start.10
  46.0 0.9 collective-permute-start.8
  46.9 3.7 %collective-permute-start.9 = (bf16[1024,128]{1,0:T(8,128)(2,1)S(1)}, bf16[1024,128]{1,0:T(8,128)(2,1)S(1)}, u32[]{:S(2)}, u32[]{:S(2)}) collective-permute-start(bf16[1024,128]{1,0:T(8,128)(2,1)S(1)} %get-tuple-element.88), channel_id=1, source_target_pairs={{0,4},{2,6},{4,0},{6,2},{1,5},{3,7},{5,1},{7,3},{8,12},{10,14},{12... | collective-permute-start | bytes 786440 | tf_op jit(solution)/shard_map/ppermute | solution.py:419
  50.7 2.7 %shard_map.102 = (f32[256,512]{1,0:T(8,128)S(1)}, f32[256,512]{1,0:T(8,128)S(1)}, f32[256,512]{1,0:T(8,128)S(1)}) custom-call(s32[5]{0:T(128)S(1)} %stack.23.refs_0_.place_ref, s32[4]{0:T(128)S(1)} %bitcast.23, f32[8,2,256]{2,1,0:T(2,128)S(1)} %get-tuple-element.68.refs_2_, bf16[256,2048]{1,0:T(8,128)(2,1)S(1)} %get-tuple-element.70.refs_3_, ...), custom_call_target="tpu_custom_call" | custom-call | flops 2147483648 | bytes 1 | tf_op jit(solution)/shard_map/pallas_call | solution.py:387
  53.9 0.9 collective-permute-start.13
  55.8 3.6 %collective-permute-done.9.refs_2_ = bf16[1024,128]{1,0:T(8,128)(2,1)S(1)} collective-permute-done((bf16[1024,128]{1,0:T(8,128)(2,1)S(1)}, bf16[1024,128]{1,0:T(8,128)(2,1)S(1)}, u32[]{:S(2)}, u32[]{:S(2)}) %collective-permute-start.9) | collective-permute-done | bytes 262176 | tf_op jit(solution)/shard_map/ppermute | solution.py:419
  59.3 1.5 %shard_map.109 = (bf16[4,256,256]{2,1,0:T(8,128)(2,1)S(1)}, bf16[5,256,256]{2,1,0:T(8,128)(2,1)S(1)}) custom-call(s32[5]{0:T(128)S(1)} %stack.23.refs_0_.place_ref, s32[4]{0:T(128)S(1)} %bitcast.24, f32[8,2,256]{2,1,0:T(2,128)S(1)} %get-tuple-element.68.refs_2_, bf16[256,2048]{1,0:T(8,128)(2,1)S(1)} %get-tuple-element.71.refs_4_.refs_3_, ...), custom_call_target="tpu_custom_call" | custom-call | flops 8589934592 | bytes 1 | tf_op jit(solution)/shard_map/pallas_call | solution.py:366
  63.1 4.2 %collective-permute-start.19 = (bf16[256,256]{1,0:T(8,128)(2,1)S(1)}, bf16[256,256]{1,0:T(8,128)(2,1)S(1)}, u32[]{:S(2)}, u32[]{:S(2)}) collective-permute-start(bf16[256,256]{1,0:T(8,128)(2,1)S(1)} %get-tuple-element.102), channel_id=1, source_target_pairs={{0,128},{1,129},{32,160},{33,161},{64,192},{65,193},{96,224},{97,2... | collective-permute-start | bytes 393224 | tf_op jit(solution)/shard_map/ppermute | solution.py:438
  67.2 1.5 %shard_map.111 = (bf16[128,2048]{1,0:T(8,128)(2,1)S(1)}, bf16[128,2048]{1,0:T(8,128)(2,1)S(1)}) custom-call(s32[5]{0:T(128)S(1)} %stack.23.refs_0_.place_ref, s32[4]{0:T(128)S(1)} %bitcast.25, f32[8,2,256]{2,1,0:T(2,128)S(1)} %get-tuple-element.68.refs_2_, bf16[256,2048]{1,0:T(8,128)(2,1)S(1)} %get-tuple-element.72.refs_5_.refs_3_, ...), custom_call_target="tpu_custom_call" | custom-call | flops 536870912 | bytes 1 | tf_op jit(solution)/shard_map/pallas_call | solution.py:366
  68.7 9.6 %collective-permute-done.13.refs_1_.refs_4_ = bf16[2,1536,256]{2,1,0:T(8,128)(2,1)S(1)} collective-permute-done((bf16[2,1536,256]{2,1,0:T(8,128)(2,1)S(1)}, bf16[2,1536,256]{2,1,0:T(8,128)(2,1)S(1)}, u32[]{:S(2)}, u32[]{:S(2)}) %collective-permute-start.13) | collective-permute-done | bytes 1572896 | tf_op jit(solution)/shard_map/ppermute | solution.py:438
  79.8 6.6 %collective-permute-start.23 = (bf16[2,256,256]{2,1,0:T(8,128)(2,1)S(1)}, bf16[2,256,256]{2,1,0:T(8,128)(2,1)S(1)}, u32[]{:S(2)}, u32[]{:S(2)}) collective-permute-start(bf16[2,256,256]{2,1,0:T(8,128)(2,1)S(1)} %get-tuple-element.104), channel_id=1, source_target_pairs={{0,64},{1,193},{32,96},{33,225},{64,128},{65,1},{96,160},{97,33},{... | collective-permute-start | bytes 786440 | tf_op jit(solution)/shard_map/ppermute | solution.py:438
  86.4 4.0 %collective-permute-start.25 = (bf16[2,256,256]{2,1,0:T(8,128)(2,1)S(1)}, bf16[2,256,256]{2,1,0:T(8,128)(2,1)S(1)}, u32[]{:S(2)}, u32[]{:S(2)}) collective-permute-start(bf16[2,256,256]{2,1,0:T(8,128)(2,1)S(1)} %get-tuple-element.105), channel_id=1, source_target_pairs={{0,96},{1,161},{32,128},{33,193},{64,160},{65,225},{96,192},{97,1}... | collective-permute-start | bytes 786440 | tf_op jit(solution)/shard_map/ppermute | solution.py:438
  90.5 11.9 %collective-permute-done.23.refs_14_ = bf16[2,256,256]{2,1,0:T(8,128)(2,1)S(1)} collective-permute-done((bf16[2,256,256]{2,1,0:T(8,128)(2,1)S(1)}, bf16[2,256,256]{2,1,0:T(8,128)(2,1)S(1)}, u32[]{:S(2)}, u32[]{:S(2)}) %collective-permute-start.23) | collective-permute-done | bytes 262176 | tf_op jit(solution)/shard_map/ppermute | solution.py:438
  102.4 6.8 %collective-permute-done.25.refs_16_ = bf16[2,256,256]{2,1,0:T(8,128)(2,1)S(1)} collective-permute-done((bf16[2,256,256]{2,1,0:T(8,128)(2,1)S(1)}, bf16[2,256,256]{2,1,0:T(8,128)(2,1)S(1)}, u32[]{:S(2)}, u32[]{:S(2)}) %collective-permute-start.25) | collective-permute-done | bytes 262176 | tf_op jit(solution)/shard_map/ppermute | solution.py:438
  109.8 0.9 collective-permute-done.22.refs_13_
  111.5 4.1 %shard_map.113 = (bf16[4,96,512]{2,1,0:T(8,128)(2,1)S(1)}, bf16[4,96,512]{2,1,0:T(8,128)(2,1)S(1)}, bf16[4,96,512]{2,1,0:T(8,128)(2,1)S(1)}, bf16[4,96,512]{2,1,0:T(8,128)(2,1)S(1)}) custom-call(s32[5]{0:T(128)S(1)} %stack.23.refs_0_.place_ref, bf16[2,1536,256]{2,1,0:T(8,128)(2,1)S(1)} %shard_map.95.refs_6_.refs_1_, ...), custom_call_target="tpu_custom_call" | custom-call | flops 1 | bytes 1 | tf_op jit(solution)/shard_map/pallas_call | solution.py:366
  115.6 1.4 collective-permute-start.28
  117.0 1.6 %collective-permute-start.29 = (bf16[4,96,512]{2,1,0:T(8,128)(2,1)S(1)}, bf16[4,96,512]{2,1,0:T(8,128)(2,1)S(1)}, u32[]{:S(2)}, u32[]{:S(2)}) collective-permute-start(bf16[4,96,512]{2,1,0:T(8,128)(2,1)S(1)} %get-tuple-element.110), channel_id=1, source_target_pairs={{0,4},{1,17},{2,6},{3,19},{4,0},{5,21},{6,2},{7,23},{8,12},{9,25},... | collective-permute-start | bytes 1179656 | tf_op jit(solution)/shard_map/ppermute | solution.py:438
  118.5 1.5 %collective-permute-start.30 = (bf16[4,96,512]{2,1,0:T(8,128)(2,1)S(1)}, bf16[4,96,512]{2,1,0:T(8,128)(2,1)S(1)}, u32[]{:S(2)}, u32[]{:S(2)}) collective-permute-start(bf16[4,96,512]{2,1,0:T(8,128)(2,1)S(1)} %get-tuple-element.111), channel_id=1, source_target_pairs={{0,6},{1,25},{2,0},{3,27},{4,2},{5,29},{6,4},{7,31},{8,14},{9,1},{... | collective-permute-start | bytes 1179656 | tf_op jit(solution)/shard_map/ppermute | solution.py:438
  120.1 1.5 %shard_map.114 = (bf16[128,2048]{1,0:T(8,128)(2,1)S(1)}, bf16[128,2048]{1,0:T(8,128)(2,1)S(1)}) custom-call(s32[5]{0:T(128)S(1)} %stack.23.refs_0_.place_ref, s32[4]{0:T(128)S(1)} %bitcast.26, f32[8,2,256]{2,1,0:T(2,128)S(1)} %get-tuple-element.68.refs_2_, bf16[256,2048]{1,0:T(8,128)(2,1)S(1)} %get-tuple-element.69.refs_6_.refs_3_, ...), custom_call_target="tpu_custom_call" | custom-call | flops 8589934592 | bytes 1 | tf_op jit(solution)/shard_map/pallas_call | solution.py:366
  122.4 2.2 %shard_map.115.refs_4_ = bf16[128,4096]{1,0:T(8,128)(2,1)} custom-call(s32[5]{0:T(128)S(1)} %stack.23.refs_0_.place_ref, bf16[128,2048]{1,0:T(8,128)(2,1)S(1)} %get-tuple-element.112.keep_ref, bf16[128,2048]{1,0:T(8,128)(2,1)S(1)} %collective-permute-done.31.other_ref, bf16[4,96,512]{2,1,0:T(8,128)(2,1)S(1)} %get-tuple-element.106.refs_10_.refs_0_), custom_call_target="tpu_custom_call" | custom-call | flops 8589934592 | bytes 1 | tf_op jit(solution)/shard_map/pallas_call | solution.py:405
  124.5 1.8 %collective-permute-done.29.refs_2_ = bf16[4,96,512]{2,1,0:T(8,128)(2,1)S(1)} collective-permute-done((bf16[4,96,512]{2,1,0:T(8,128)(2,1)S(1)}, bf16[4,96,512]{2,1,0:T(8,128)(2,1)S(1)}, u32[]{:S(2)}, u32[]{:S(2)}) %collective-permute-start.29) | collective-permute-done | bytes 393248 | tf_op jit(solution)/shard_map/ppermute | solution.py:438
  126.3 4.1 %collective-permute-done.30.refs_3_ = bf16[4,96,512]{2,1,0:T(8,128)(2,1)S(1)} collective-permute-done((bf16[4,96,512]{2,1,0:T(8,128)(2,1)S(1)}, bf16[4,96,512]{2,1,0:T(8,128)(2,1)S(1)}, u32[]{:S(2)}, u32[]{:S(2)}) %collective-permute-start.30) | collective-permute-done | bytes 393248 | tf_op jit(solution)/shard_map/ppermute | solution.py:438
  130.4 1.2 copy-done
  132.5 1.7 %collective-permute-start.32 = (bf16[96,512]{1,0:T(8,128)(2,1)S(1)}, bf16[96,512]{1,0:T(8,128)(2,1)S(1)}, u32[]{:S(2)}, u32[]{:S(2)}) collective-permute-start(bf16[96,512]{1,0:T(8,128)(2,1)S(1)} %get-tuple-element.118), channel_id=1, source_target_pairs={{0,8},{1,3},{2,10},{3,5},{4,12},{5,7},{6,14},{7,1},{8,16},{9,11},{... | collective-permute-start | bytes 294920 | tf_op jit(solution)/shard_map/ppermute | solution.py:438
  134.2 2.9 %collective-permute-start.33 = (bf16[96,512]{1,0:T(8,128)(2,1)S(1)}, bf16[96,512]{1,0:T(8,128)(2,1)S(1)}, u32[]{:S(2)}, u32[]{:S(2)}) collective-permute-start(bf16[96,512]{1,0:T(8,128)(2,1)S(1)} %get-tuple-element.119), channel_id=1, source_target_pairs={{0,16},{1,5},{2,18},{3,7},{4,20},{5,1},{6,22},{7,3},{8,24},{9,13},... | collective-permute-start | bytes 294920 | tf_op jit(solution)/shard_map/ppermute | solution.py:438
  137.1 1.3 collective-permute-start.34
  138.4 2.2 %shard_map.118.refs_4_ = bf16[128,4096]{1,0:T(8,128)(2,1)} custom-call(s32[5]{0:T(128)S(1)} %stack.23.refs_0_.place_ref, bf16[128,2048]{1,0:T(8,128)(2,1)S(1)} %get-tuple-element.107.keep_ref, bf16[128,2048]{1,0:T(8,128)(2,1)S(1)} %collective-permute-done.27.other_ref, bf16[96,512]{1,0:T(8,128)(2,1)S(1)} %get-tuple-element.117.refs_0_), custom_call_target="tpu_custom_call" | custom-call | flops 8589934592 | bytes 1 | tf_op jit(solution)/shard_map/pallas_call | solution.py:405
  140.7 1.0 collective-permute-done.34.refs_3_
  141.7 1.2 copy-done.1
  (68 shorter events, 12.0 us)
Async XLA Ops:
  0.6 1.1 copy-start.2
  1.8 3.6 %copy-start.7 = (bf16[1,128,4096]{2,1,0:T(8,128)(2,1)S(1)}, bf16[1,128,4096]{2,1,0:T(8,128)(2,1)}, u32[]{:S(2)}) copy-start(bf16[1,128,4096]{2,1,0:T(8,128)(2,1)} %param.10) | copy-start | bytes 3145732
  1.8 3.6 %copy-start.8 = (f32[1,32,128]{2,1,0:T(8,128)S(1)}, f32[1,32,128]{2,1,0:T(8,128)}, u32[]{:S(2)}) copy-start(f32[1,32,128]{2,1,0:T(8,128)} %param.12) | copy-start | bytes 49156
  2.1 2.4 %collective-permute-start = (bf16[2,16,96,128]{3,2,1,0:T(8,128)(2,1)S(1)}, bf16[2,16,96,128]{3,2,1,0:T(8,128)(2,1)S(1)}, u32[]{:S(2)}, u32[]{:S(2)}) collective-permute-start(bf16[2,16,96,128]{3,2,1,0:T(8,128)(2,1)S(1)} %shard_map.94), channel_id=1, source_target_pairs={{0,1},{1,0},{2,3},{3,2},{4,5},{5,4},{6,7},{7,6},{8,9},{9,8},{10,11... | collective-permute-start | bytes 2359304 | tf_op jit(solution)/shard_map/ppermute | solution.py:419
  4.5 1.2 copy-start.4
  4.5 1.5 %copy-start.5 = (bf16[1,128,4096]{2,1,0:T(8,128)(2,1)S(1)}, bf16[1,128,4096]{2,1,0:T(8,128)(2,1)}, u32[]{:S(2)}) copy-start(bf16[1,128,4096]{2,1,0:T(8,128)(2,1)} %param.11) | copy-start | bytes 3145732
  4.5 1.9 %copy-start.6 = (bf16[1,128,4096]{2,1,0:T(8,128)(2,1)S(1)}, bf16[1,128,4096]{2,1,0:T(8,128)(2,1)}, u32[]{:S(2)}) copy-start(bf16[1,128,4096]{2,1,0:T(8,128)(2,1)} %param.9) | copy-start | bytes 3145732
  6.4 5.4 %copy-start.3 = (s32[1,4]{1,0:T(1,128)S(1)}, s32[1,4]{1,0:T(1,128)}, u32[]{:S(2)}) copy-start(s32[1,4]{1,0:T(1,128)} %param.13) | copy-start | bytes 52
  7.5 4.3 %collective-permute-start.2 = (bf16[4,128,2048]{2,1,0:T(8,128)(2,1)S(1)}, bf16[4,128,2048]{2,1,0:T(8,128)(2,1)S(1)}, u32[]{:S(2)}, u32[]{:S(2)}) collective-permute-start(bf16[4,128,2048]{2,1,0:T(8,128)(2,1)S(1)} %get-tuple-element.67), channel_id=1, source_target_pairs={{0,1},{1,0},{2,3},{3,2},{4,5},{5,4},{6,7},{7,6},{8,9},{9,8},{10,11... | collective-permute-start | bytes 6291464 | tf_op jit(solution)/shard_map/ppermute | solution.py:419
  7.7 24.8 %collective-permute-start.11 = (bf16[2,1536,256]{2,1,0:T(8,128)(2,1)S(1)}, bf16[2,1536,256]{2,1,0:T(8,128)(2,1)S(1)}, u32[]{:S(2)}, u32[]{:S(2)}) collective-permute-start(bf16[2,1536,256]{2,1,0:T(8,128)(2,1)S(1)} %shard_map.95.refs_6_.refs_1_), channel_id=1, source_target_pairs={{0,32},{1,225},{32,64},{33,1},{64,96},{65,33},{96,128},{97,65},{12... | collective-permute-start | bytes 4718600 | tf_op jit(solution)/shard_map/ppermute | solution.py:438
  9.7 2.1 %collective-permute-start.1 = (f32[16,128]{1,0:T(8,128)S(1)}, f32[16,128]{1,0:T(8,128)S(1)}, u32[]{:S(2)}, u32[]{:S(2)}) collective-permute-start(f32[16,128]{1,0:T(8,128)S(1)} %get-tuple-element.65), channel_id=1, source_target_pairs={{0,1},{1,0},{2,3},{3,2},{4,5},{5,4},{6,7},{7,6},{8,9},{9,8},{10,11... | collective-permute-start | bytes 24584 | tf_op jit(solution)/shard_map/ppermute | solution.py:419
  16.2 11.9 %collective-permute-start.3 = (bf16[1040,128]{1,0:T(8,128)(2,1)S(1)}, bf16[1040,128]{1,0:T(8,128)(2,1)S(1)}, u32[]{:S(2)}, u32[]{:S(2)}) collective-permute-start(bf16[1040,128]{1,0:T(8,128)(2,1)S(1)} %get-tuple-element.75), channel_id=1, source_target_pairs={{0,2},{2,4},{4,6},{6,0},{1,3},{3,5},{5,7},{7,1},{8,10},{10,12},{12... | collective-permute-start | bytes 798728 | tf_op jit(solution)/shard_map/ppermute | solution.py:419
  17.8 10.8 %collective-permute-start.4 = (bf16[1040,128]{1,0:T(8,128)(2,1)S(1)}, bf16[1040,128]{1,0:T(8,128)(2,1)S(1)}, u32[]{:S(2)}, u32[]{:S(2)}) collective-permute-start(bf16[1040,128]{1,0:T(8,128)(2,1)S(1)} %get-tuple-element.76), channel_id=1, source_target_pairs={{0,4},{2,6},{4,0},{6,2},{1,5},{3,7},{5,1},{7,3},{8,12},{10,14},{12... | collective-permute-start | bytes 798728 | tf_op jit(solution)/shard_map/ppermute | solution.py:419
  18.9 13.6 %collective-permute-start.5 = (bf16[1040,128]{1,0:T(8,128)(2,1)S(1)}, bf16[1040,128]{1,0:T(8,128)(2,1)S(1)}, u32[]{:S(2)}, u32[]{:S(2)}) collective-permute-start(bf16[1040,128]{1,0:T(8,128)(2,1)S(1)} %get-tuple-element.77), channel_id=1, source_target_pairs={{0,6},{2,0},{4,2},{6,4},{1,7},{3,1},{5,3},{7,5},{8,14},{10,8},{12,... | collective-permute-start | bytes 798728 | tf_op jit(solution)/shard_map/ppermute | solution.py:419
  32.5 21.5 %collective-permute-start.12 = (bf16[2,1536,256]{2,1,0:T(8,128)(2,1)S(1)}, bf16[2,1536,256]{2,1,0:T(8,128)(2,1)S(1)}, u32[]{:S(2)}, u32[]{:S(2)}) collective-permute-start(bf16[2,1536,256]{2,1,0:T(8,128)(2,1)S(1)} %shard_map.103.refs_1_.refs_2_), channel_id=1, source_target_pairs={{0,32},{1,225},{32,64},{33,1},{64,96},{65,33},{96,128},{97,65},{12... | collective-permute-start | bytes 4718600 | tf_op jit(solution)/shard_map/ppermute | solution.py:438
  35.3 7.4 %collective-permute-start.6 = (bf16[512,128]{1,0:T(8,128)(2,1)S(1)}, bf16[512,128]{1,0:T(8,128)(2,1)S(1)}, u32[]{:S(2)}, u32[]{:S(2)}) collective-permute-start(bf16[512,128]{1,0:T(8,128)(2,1)S(1)} %get-tuple-element.83), channel_id=1, source_target_pairs={{8,0},{16,8},{24,16},{9,1},{17,9},{25,17},{10,2},{18,10},{26,18},{... | collective-permute-start | bytes 393224 | tf_op jit(solution)/shard_map/ppermute | solution.py:488
  36.6 7.3 %collective-permute-start.7 = (bf16[512,128]{1,0:T(8,128)(2,1)S(1)}, bf16[512,128]{1,0:T(8,128)(2,1)S(1)}, u32[]{:S(2)}, u32[]{:S(2)}) collective-permute-start(bf16[512,128]{1,0:T(8,128)(2,1)S(1)} %get-tuple-element.84), channel_id=1, source_target_pairs={{0,8},{8,16},{16,24},{1,9},{9,17},{17,25},{2,10},{10,18},{18,26},{... | collective-permute-start | bytes 393224 | tf_op jit(solution)/shard_map/ppermute | solution.py:489
  44.8 10.7 %collective-permute-start.10 = (bf16[1024,128]{1,0:T(8,128)(2,1)S(1)}, bf16[1024,128]{1,0:T(8,128)(2,1)S(1)}, u32[]{:S(2)}, u32[]{:S(2)}) collective-permute-start(bf16[1024,128]{1,0:T(8,128)(2,1)S(1)} %get-tuple-element.89), channel_id=1, source_target_pairs={{0,6},{2,0},{4,2},{6,4},{1,7},{3,1},{5,3},{7,5},{8,14},{10,8},{12,... | collective-permute-start | bytes 786440 | tf_op jit(solution)/shard_map/ppermute | solution.py:419
  46.0 9.7 %collective-permute-start.8 = (bf16[1024,128]{1,0:T(8,128)(2,1)S(1)}, bf16[1024,128]{1,0:T(8,128)(2,1)S(1)}, u32[]{:S(2)}, u32[]{:S(2)}) collective-permute-start(bf16[1024,128]{1,0:T(8,128)(2,1)S(1)} %get-tuple-element.87), channel_id=1, source_target_pairs={{0,2},{2,4},{4,6},{6,0},{1,3},{3,5},{5,7},{7,1},{8,10},{10,12},{12... | collective-permute-start | bytes 786440 | tf_op jit(solution)/shard_map/ppermute | solution.py:419
  46.9 12.4 %collective-permute-start.9 = (bf16[1024,128]{1,0:T(8,128)(2,1)S(1)}, bf16[1024,128]{1,0:T(8,128)(2,1)S(1)}, u32[]{:S(2)}, u32[]{:S(2)}) collective-permute-start(bf16[1024,128]{1,0:T(8,128)(2,1)S(1)} %get-tuple-element.88), channel_id=1, source_target_pairs={{0,4},{2,6},{4,0},{6,2},{1,5},{3,7},{5,1},{7,3},{8,12},{10,14},{12... | collective-permute-start | bytes 786440 | tf_op jit(solution)/shard_map/ppermute | solution.py:419
  53.9 24.4 %collective-permute-start.13 = (bf16[2,1536,256]{2,1,0:T(8,128)(2,1)S(1)}, bf16[2,1536,256]{2,1,0:T(8,128)(2,1)S(1)}, u32[]{:S(2)}, u32[]{:S(2)}) collective-permute-start(bf16[2,1536,256]{2,1,0:T(8,128)(2,1)S(1)} %shard_map.104.refs_4_.refs_1_.refs_3_), channel_id=1, source_target_pairs={{0,32},{1,225},{32,64},{33,1},{64,96},{65,33},{96,128},{97,65},{12... | collective-permute-start | bytes 4718600 | tf_op jit(solution)/shard_map/ppermute | solution.py:438
  55.4 24.3 %collective-permute-start.14 = (bf16[1536,256]{1,0:T(8,128)(2,1)S(1)}, bf16[1536,256]{1,0:T(8,128)(2,1)S(1)}, u32[]{:S(2)}, u32[]{:S(2)}) collective-permute-start(bf16[1536,256]{1,0:T(8,128)(2,1)S(1)} %shard_map.106), channel_id=1, source_target_pairs={{0,1},{1,0},{2,3},{3,2},{4,5},{5,4},{6,7},{7,6},{8,9},{9,8},{10,11... | collective-permute-start | bytes 2359304 | tf_op jit(solution)/shard_map/ppermute | solution.py:419
  60.9 2.0 %collective-permute-start.17 = (bf16[4,256,256]{2,1,0:T(8,128)(2,1)S(1)}, bf16[4,256,256]{2,1,0:T(8,128)(2,1)S(1)}, u32[]{:S(2)}, u32[]{:S(2)}) collective-permute-start(bf16[4,256,256]{2,1,0:T(8,128)(2,1)S(1)} %get-tuple-element.99), channel_id=1, source_target_pairs={{0,1},{1,0},{2,3},{3,2},{4,5},{5,4},{6,7},{7,6},{8,9},{9,8},{10,11... | collective-permute-start | bytes 1572872 | tf_op jit(solution)/shard_map/ppermute | solution.py:419
  61.6 48.1 %collective-permute-start.15 = (bf16[1536,256]{1,0:T(8,128)(2,1)S(1)}, bf16[1536,256]{1,0:T(8,128)(2,1)S(1)}, u32[]{:S(2)}, u32[]{:S(2)}) collective-permute-start(bf16[1536,256]{1,0:T(8,128)(2,1)S(1)} %shard_map.107), channel_id=1, source_target_pairs={{0,1},{1,0},{2,3},{3,2},{4,5},{5,4},{6,7},{7,6},{8,9},{9,8},{10,11... | collective-permute-start | bytes 2359304 | tf_op jit(solution)/shard_map/ppermute | solution.py:419
  63.0 23.5 %collective-permute-start.21 = (bf16[2,256,256]{2,1,0:T(8,128)(2,1)S(1)}, bf16[2,256,256]{2,1,0:T(8,128)(2,1)S(1)}, u32[]{:S(2)}, u32[]{:S(2)}) collective-permute-start(bf16[2,256,256]{2,1,0:T(8,128)(2,1)S(1)} %get-tuple-element.100.refs_10_), channel_id=1, source_target_pairs={{0,32},{1,225},{32,64},{33,1},{64,96},{65,33},{96,128},{97,65},{12... | collective-permute-start | bytes 786440 | tf_op jit(solution)/shard_map/ppermute | solution.py:438
  63.1 16.7 %collective-permute-start.19 = (bf16[256,256]{1,0:T(8,128)(2,1)S(1)}, bf16[256,256]{1,0:T(8,128)(2,1)S(1)}, u32[]{:S(2)}, u32[]{:S(2)}) collective-permute-start(bf16[256,256]{1,0:T(8,128)(2,1)S(1)} %get-tuple-element.102), channel_id=1, source_target_pairs={{0,128},{1,129},{32,160},{33,161},{64,192},{65,193},{96,224},{97,2... | collective-permute-start | bytes 393224 | tf_op jit(solution)/shard_map/ppermute | solution.py:438
  79.0 32.5 %collective-permute-start.18 = (bf16[1536,256]{1,0:T(8,128)(2,1)S(1)}, bf16[1536,256]{1,0:T(8,128)(2,1)S(1)}, u32[]{:S(2)}, u32[]{:S(2)}) collective-permute-start(bf16[1536,256]{1,0:T(8,128)(2,1)S(1)} %shard_map.112), channel_id=1, source_target_pairs={{0,32},{1,225},{32,64},{33,1},{64,96},{65,33},{96,128},{97,65},{12... | collective-permute-start | bytes 2359304 | tf_op jit(solution)/shard_map/ppermute | solution.py:438
  79.7 31.8 %collective-permute-start.16 = (bf16[1536,256]{1,0:T(8,128)(2,1)S(1)}, bf16[1536,256]{1,0:T(8,128)(2,1)S(1)}, u32[]{:S(2)}, u32[]{:S(2)}) collective-permute-start(bf16[1536,256]{1,0:T(8,128)(2,1)S(1)} %shard_map.108), channel_id=1, source_target_pairs={{0,1},{1,0},{2,3},{3,2},{4,5},{5,4},{6,7},{7,6},{8,9},{9,8},{10,11... | collective-permute-start | bytes 2359304 | tf_op jit(solution)/shard_map/ppermute | solution.py:419
  79.8 22.6 %collective-permute-start.23 = (bf16[2,256,256]{2,1,0:T(8,128)(2,1)S(1)}, bf16[2,256,256]{2,1,0:T(8,128)(2,1)S(1)}, u32[]{:S(2)}, u32[]{:S(2)}) collective-permute-start(bf16[2,256,256]{2,1,0:T(8,128)(2,1)S(1)} %get-tuple-element.104), channel_id=1, source_target_pairs={{0,64},{1,193},{32,96},{33,225},{64,128},{65,1},{96,160},{97,33},{... | collective-permute-start | bytes 786440 | tf_op jit(solution)/shard_map/ppermute | solution.py:438
  86.4 22.7 %collective-permute-start.25 = (bf16[2,256,256]{2,1,0:T(8,128)(2,1)S(1)}, bf16[2,256,256]{2,1,0:T(8,128)(2,1)S(1)}, u32[]{:S(2)}, u32[]{:S(2)}) collective-permute-start(bf16[2,256,256]{2,1,0:T(8,128)(2,1)S(1)} %get-tuple-element.105), channel_id=1, source_target_pairs={{0,96},{1,161},{32,128},{33,193},{64,160},{65,225},{96,192},{97,1}... | collective-permute-start | bytes 786440 | tf_op jit(solution)/shard_map/ppermute | solution.py:438
  102.4 6.8 %collective-permute-start.20 = (bf16[256,256]{1,0:T(8,128)(2,1)S(1)}, bf16[256,256]{1,0:T(8,128)(2,1)S(1)}, u32[]{:S(2)}, u32[]{:S(2)}) collective-permute-start(bf16[256,256]{1,0:T(8,128)(2,1)S(1)} %collective-permute-done.19.refs_9_), channel_id=1, source_target_pairs={{0,1},{1,0},{2,3},{3,2},{4,5},{5,4},{6,7},{7,6},{8,9},{9,8},{10,11... | collective-permute-start | bytes 393224 | tf_op jit(solution)/shard_map/ppermute | solution.py:419
  109.2 1.5 %collective-permute-start.22 = (bf16[2,256,256]{2,1,0:T(8,128)(2,1)S(1)}, bf16[2,256,256]{2,1,0:T(8,128)(2,1)S(1)}, u32[]{:S(2)}, u32[]{:S(2)}) collective-permute-start(bf16[2,256,256]{2,1,0:T(8,128)(2,1)S(1)} %collective-permute-done.21.refs_12_), channel_id=1, source_target_pairs={{0,1},{1,0},{2,3},{3,2},{4,5},{5,4},{6,7},{7,6},{8,9},{9,8},{10,11... | collective-permute-start | bytes 786440 | tf_op jit(solution)/shard_map/ppermute | solution.py:419
  109.2 1.9 %collective-permute-start.24 = (bf16[2,256,256]{2,1,0:T(8,128)(2,1)S(1)}, bf16[2,256,256]{2,1,0:T(8,128)(2,1)S(1)}, u32[]{:S(2)}, u32[]{:S(2)}) collective-permute-start(bf16[2,256,256]{2,1,0:T(8,128)(2,1)S(1)} %collective-permute-done.23.refs_14_), channel_id=1, source_target_pairs={{0,1},{1,0},{2,3},{3,2},{4,5},{5,4},{6,7},{7,6},{8,9},{9,8},{10,11... | collective-permute-start | bytes 786440 | tf_op jit(solution)/shard_map/ppermute | solution.py:419
  109.7 1.8 %collective-permute-start.26 = (bf16[2,256,256]{2,1,0:T(8,128)(2,1)S(1)}, bf16[2,256,256]{2,1,0:T(8,128)(2,1)S(1)}, u32[]{:S(2)}, u32[]{:S(2)}) collective-permute-start(bf16[2,256,256]{2,1,0:T(8,128)(2,1)S(1)} %collective-permute-done.25.refs_16_), channel_id=1, source_target_pairs={{0,1},{1,0},{2,3},{3,2},{4,5},{5,4},{6,7},{7,6},{8,9},{9,8},{10,11... | collective-permute-start | bytes 786440 | tf_op jit(solution)/shard_map/ppermute | solution.py:419
  110.7 11.6 %collective-permute-start.31 = (bf16[128,2048]{1,0:T(8,128)(2,1)S(1)}, bf16[128,2048]{1,0:T(8,128)(2,1)S(1)}, u32[]{:S(2)}, u32[]{:S(2)}) collective-permute-start(bf16[128,2048]{1,0:T(8,128)(2,1)S(1)} %get-tuple-element.101.refs_2_.refs_18_), channel_id=1, source_target_pairs={{0,1},{1,0},{2,3},{3,2},{4,5},{5,4},{6,7},{7,6},{8,9},{9,8},{10,11... | collective-permute-start | bytes 1572872 | tf_op jit(solution)/shard_map/ppermute | solution.py:419
  115.6 9.0 %collective-permute-start.28 = (bf16[4,96,512]{2,1,0:T(8,128)(2,1)S(1)}, bf16[4,96,512]{2,1,0:T(8,128)(2,1)S(1)}, u32[]{:S(2)}, u32[]{:S(2)}) collective-permute-start(bf16[4,96,512]{2,1,0:T(8,128)(2,1)S(1)} %get-tuple-element.109), channel_id=1, source_target_pairs={{0,2},{1,9},{2,4},{3,11},{4,6},{5,13},{6,0},{7,15},{8,10},{9,17},{... | collective-permute-start | bytes 1179656 | tf_op jit(solution)/shard_map/ppermute | solution.py:438
  117.0 9.4 %collective-permute-start.29 = (bf16[4,96,512]{2,1,0:T(8,128)(2,1)S(1)}, bf16[4,96,512]{2,1,0:T(8,128)(2,1)S(1)}, u32[]{:S(2)}, u32[]{:S(2)}) collective-permute-start(bf16[4,96,512]{2,1,0:T(8,128)(2,1)S(1)} %get-tuple-element.110), channel_id=1, source_target_pairs={{0,4},{1,17},{2,6},{3,19},{4,0},{5,21},{6,2},{7,23},{8,12},{9,25},... | collective-permute-start | bytes 1179656 | tf_op jit(solution)/shard_map/ppermute | solution.py:438
  118.5 11.9 %collective-permute-start.30 = (bf16[4,96,512]{2,1,0:T(8,128)(2,1)S(1)}, bf16[4,96,512]{2,1,0:T(8,128)(2,1)S(1)}, u32[]{:S(2)}, u32[]{:S(2)}) collective-permute-start(bf16[4,96,512]{2,1,0:T(8,128)(2,1)S(1)} %get-tuple-element.111), channel_id=1, source_target_pairs={{0,6},{1,25},{2,0},{3,27},{4,2},{5,29},{6,4},{7,31},{8,14},{9,1},{... | collective-permute-start | bytes 1179656 | tf_op jit(solution)/shard_map/ppermute | solution.py:438
  121.5 16.9 %collective-permute-start.27 = (bf16[128,2048]{1,0:T(8,128)(2,1)S(1)}, bf16[128,2048]{1,0:T(8,128)(2,1)S(1)}, u32[]{:S(2)}, u32[]{:S(2)}) collective-permute-start(bf16[128,2048]{1,0:T(8,128)(2,1)S(1)} %get-tuple-element.108), channel_id=1, source_target_pairs={{0,1},{1,0},{2,3},{3,2},{4,5},{5,4},{6,7},{7,6},{8,9},{9,8},{10,11... | collective-permute-start | bytes 1572872 | tf_op jit(solution)/shard_map/ppermute | solution.py:419
  130.4 1.2 copy-start
  132.5 8.1 %collective-permute-start.32 = (bf16[96,512]{1,0:T(8,128)(2,1)S(1)}, bf16[96,512]{1,0:T(8,128)(2,1)S(1)}, u32[]{:S(2)}, u32[]{:S(2)}) collective-permute-start(bf16[96,512]{1,0:T(8,128)(2,1)S(1)} %get-tuple-element.118), channel_id=1, source_target_pairs={{0,8},{1,3},{2,10},{3,5},{4,12},{5,7},{6,14},{7,1},{8,16},{9,11},{... | collective-permute-start | bytes 294920 | tf_op jit(solution)/shard_map/ppermute | solution.py:438
  134.2 6.5 %collective-permute-start.33 = (bf16[96,512]{1,0:T(8,128)(2,1)S(1)}, bf16[96,512]{1,0:T(8,128)(2,1)S(1)}, u32[]{:S(2)}, u32[]{:S(2)}) collective-permute-start(bf16[96,512]{1,0:T(8,128)(2,1)S(1)} %get-tuple-element.119), channel_id=1, source_target_pairs={{0,16},{1,5},{2,18},{3,7},{4,20},{5,1},{6,22},{7,3},{8,24},{9,13},... | collective-permute-start | bytes 294920 | tf_op jit(solution)/shard_map/ppermute | solution.py:438
  137.1 4.6 %collective-permute-start.34 = (bf16[96,512]{1,0:T(8,128)(2,1)S(1)}, bf16[96,512]{1,0:T(8,128)(2,1)S(1)}, u32[]{:S(2)}, u32[]{:S(2)}) collective-permute-start(bf16[96,512]{1,0:T(8,128)(2,1)S(1)} %get-tuple-element.120), channel_id=1, source_target_pairs={{0,24},{1,7},{2,26},{3,1},{4,28},{5,3},{6,30},{7,5},{8,0},{9,15},{... | collective-permute-start | bytes 294920 | tf_op jit(solution)/shard_map/ppermute | solution.py:438
  141.7 1.2 copy-start.1
